TPU v7x, 512 devices: a whole 4x8x8 slice. The times are simulated.
512 devices in a mesh: mp: 32 (over z, y_lo), dp: 16 (over x, y_hi, core).
Axes of the slice: x: 4, y: 8 (y_hi: 2, y_lo: 4; y = y_hi * 4 + y_lo), z: 8, core: 2. Of those that a mesh axis runs over, the one named last changes fastest.
Arguments:
- forward_fields: bfloat16 [16, 4, 65536], P(None, None, 'mp'), may hold values from -6 to 6
- adjoint_fields: bfloat16 [64, 4, 65536], P(None, None, 'mp'), may hold values from -6 to 6
- data_rec: int32 [3072], P('dp'), may hold values from 0 to 63
- data_freq: int32 [3072], P('dp'), may hold values from 0 to 15
- data_coef: float32 [3072, 4], P('dp'), may hold values from -6 to 6
- residual_cols: bfloat16 [3072, 256], P('dp'), may hold values from -6 to 6
Outputs:
- data_update: bfloat16 [3072, 256], P('dp')
- model_update: float32 [65536, 256], P(('mp', 'dp'))
All inputs are finite; a program needn't handle non-finite values.
Results may differ from a plain program's by a relative error of at most 0.0075.
Values may be sent and summed in bfloat16 or wider, within the bound.
No kernel may reach another device: no remote copies, remote signals or barrier semaphores. Data moves between devices by JAX's collectives and lax.ppermute only.
A program may use at most 64 MiB of HBM per device.

v0:
```python
import math

import jax
import jax.numpy as jnp
from jax import lax
from jax.sharding import PartitionSpec as P

GRID_COLS = 128
SWEEPS = 2


def with_halo(array, sides, width):
    for axis, dim in sides:
        peers, length = (lax.axis_size(axis), array.shape[dim])
        up = [(i, (i + 1) % peers) for i in range(peers - 1)]
        down = [(j, i) for i, j in up]
        last = lax.slice_in_dim(array, length - width, length, axis=dim)
        leading = lax.slice_in_dim(array, 0, width, axis=dim)
        before = lax.ppermute(last, axis, up)
        after = lax.ppermute(leading, axis, down)
        array = jnp.concatenate([before, array, after], axis=dim)
    return array


def sweep_once(field):
    center = field[:, 1:-1, :]
    sides = jnp.pad(center, ((0, 0), (0, 0), (1, 1)))
    beside_all = field[:, :-2, :] + field[:, 2:, :] + sides[:, :, :-2] + sides[:, :, 2:]
    return center + 0.2 * (beside_all - 4.0 * center)


def per_device(forward_fields, adjoint_fields, data_rec, data_freq, data_coef, residual_cols):
    rows_here = data_rec.shape[0]
    cells_here = forward_fields.shape[2]
    slab_rows = cells_here // GRID_COLS
    slab_count = lax.axis_size("mp")
    block_count = lax.axis_size("dp")
    adjoint = adjoint_fields[data_rec].astype(jnp.float32)
    forward = forward_fields[data_freq].astype(jnp.float32)
    sens = (0.5 * jnp.sum(data_coef[:, :, None] * adjoint * forward, axis=1)).astype(jnp.bfloat16)
    grid = sens.astype(jnp.float32).reshape(rows_here, slab_rows, GRID_COLS)
    for sweep in range(SWEEPS):
        padded = with_halo(grid, (("mp", 1),), 1)
        grid = sweep_once(padded)
    smooth = grid.reshape(rows_here, cells_here).astype(jnp.bfloat16)
    residual_whole = lax.all_gather(residual_cols, "dp", axis=0, tiled=True)
    gram_tile = lax.dot_general(
        smooth,
        lax.all_gather(sens, "dp", axis=0, tiled=True),
        (((1,), (1,)), ((), ())),
        preferred_element_type=jnp.float32,
    )
    partial_value = jnp.dot(
        gram_tile, residual_whole.astype(jnp.float32), precision=lax.Precision.HIGHEST
    )
    gram_prod = lax.psum(partial_value, "mp") / (cells_here * slab_count)
    data_update = (gram_prod + residual_cols.astype(jnp.float32)).astype(jnp.bfloat16)
    summed = lax.psum_scatter(
        lax.dot_general(
            smooth, data_update, (((0,), (0,)), ((), ())), preferred_element_type=jnp.float32
        ),
        "dp",
        scatter_dimension=0,
        tiled=True,
    )
    model_update = summed / math.sqrt(rows_here * block_count)
    return (data_update, model_update)


def solution(mesh):
    in_specs = (
        P(None, None, "mp"),
        P(None, None, "mp"),
        P("dp"),
        P("dp"),
        P("dp", None),
        P("dp", None),
    )
    out_specs = (P("dp", None), P(("mp", "dp"), None))
    return jax.shard_map(
        per_device, mesh=mesh, in_specs=in_specs, out_specs=out_specs, check_vma=False
    )
```

profile of v0, /device:TPU:1, one launch (start us, length us, event | category | flops | bytes accessed | tf_op | source)
XLA Modules:
  0.0 661.7 jit_solution(15564410182115889151)
XLA Ops:
  7.2 0.8 compare_select_fusion.1
  8.0 0.7 compare_select_fusion
  8.7 0.8 copy.8
  9.5 9.6 %gather_fusion = bf16[192,4,2048]{2,1,0:T(4,128)(2,1)} fusion(bf16[64,4,2048]{2,1,0:T(4,128)(2,1)S(1)} %copy-done, s32[1024]{0:T(1024)S(1)} %pad_clamp_fusion.1), kind=kCustom, calls=%fused_computation | custom fusion | bytes 6292224 | tf_op jit(solution)/shard_map/gather | solution.py:38
  19.1 9.7 %gather_fusion.1 = bf16[192,4,2048]{2,1,0:T(4,128)(2,1)} fusion(bf16[16,4,2048]{2,1,0:T(4,128)(2,1)S(1)} %copy-done.1, s32[1024]{0:T(1024)S(1)} %pad_clamp_fusion), kind=kCustom, calls=%fused_computation.1 | custom fusion | bytes 6292224 | tf_op jit(solution)/shard_map/gather | solution.py:39
  28.8 9.7 %multiply_reduce_fusion = f32[192,2048]{1,0:T(8,128)S(1)} fusion(bf16[192,4,2048]{2,1,0:T(4,128)(2,1)} %gather_fusion.1, bf16[192,4,2048]{2,1,0:T(4,128)(2,1)} %gather_fusion, f32[192,4]{1,0:T(8,128)S(1)} %copy.8), kind=kLoop, calls=%fused_computation.2 | loop fusion | flops 7471104 | bytes 7867392 | tf_op jit(solution)/shard_map/reduce_sum | solution.py:40
  38.5 1.2 convert_bitcast_fusion
  39.7 0.0 all-gather.5.cloned.1.call-start
  39.7 0.7 all-gather.5.cloned.1.call-update
  40.5 0.3 copy.9
  40.8 0.1 fusion.20
  40.9 4.0 collective-permute-start
  45.0 1.3 collective-permute-start.1
  46.3 0.3 collective-permute-done
  46.6 5.8 collective-permute-done.1
  52.4 1.3 fusion.4
  53.8 0.1 fusion.19
  53.9 3.8 collective-permute-start.2
  57.7 1.5 collective-permute-start.3
  59.2 0.1 collective-permute-done.2
  59.3 6.9 %collective-permute-done.3 = f32[192,1,128]{2,1,0:T(1,128)S(1)} collective-permute-done((f32[192,1,128]{2,1,0:T(1,128)S(1)}, f32[192,1,128]{2,1,0:T(1,128)S(1)}, u32[]{:S(2)}, u32[]{:S(2)}) %collective-permute-start.3) | collective-permute-done | bytes 98336 | tf_op jit(solution)/shard_map/ppermute | solution.py:20
  66.2 1.3 fusion.10
  67.6 128.7 %all-gather.3.cloned.1.call-done = bf16[3072,2048]{1,0:T(8,128)(2,1)} async-done(((bf16[192,2048]{1,0:T(8,128)(2,1)}), bf16[3072,2048]{1,0:T(8,128)(2,1)}) %all-gather.3.cloned.1.call-update) | async-done | bytes 12582928 | tf_op jit(solution)/shard_map/all_gather | solution.py:49
  196.3 10.2 %fusion.15 = f32[192,3072]{1,0:T(8,128)} fusion(bf16[3072,2048]{1,0:T(8,128)(2,1)} %all-gather.3.cloned.1.call-done, bf16[24,8,16,128]{3,2,1,0:T(8,128)(2,1)S(1)} %bitcast.15), kind=kOutput, calls=%fused_computation.28 | convolution fusion | flops 2415919104 | bytes 15728640 | tf_op jit(solution)/shard_map/dot_general | solution.py:47
  206.5 50.8 %all-gather.5.cloned.1.call-done = bf16[3072,256]{1,0:T(8,128)(2,1)} async-done(((bf16[192,256]{1,0:T(8,128)(2,1)}), bf16[3072,256]{1,0:T(8,128)(2,1)}) %all-gather.5.cloned.1.call-update) | async-done | bytes 1572880 | tf_op jit(solution)/shard_map/all_gather | solution.py:46
  257.3 4.0 fusion.21
  261.4 0.0 reduce-scatter.2.cloned.1.call-start
  261.4 272.9 %all-reduce.4.cloned.1.call-done = f32[192,256]{1,0:T(8,128)} async-done(((f32[192,256]{1,0:T(8,128)}), f32[192,256]{1,0:T(8,128)}) %all-reduce.4.cloned.1.call-update) | async-done | bytes 196624 | tf_op jit(solution)/shard_map/psum | solution.py:56
  534.3 1.0 add_convert_fusion
  535.2 1.8 fusion.13
  537.1 116.5 %reduce-scatter.2.cloned.1.call-done = f32[128,256]{1,0:T(8,128)} async-done(((f32[2048,256]{1,0:T(8,128)}), f32[128,256]{1,0:T(8,128)}) %reduce-scatter.2.cloned.1.call-update) | async-done | bytes 131088 | tf_op jit(solution)/shard_map/reduce_scatter | solution.py:58
  653.6 1.6 broadcast_multiply_fusion
  (15 shorter events, 0.2 us)
Async XLA Ops:
  7.2 2.3 copy-start
  7.2 189.1 %all-gather.3.cloned.1.call-start = ((), (), s32[]{:S(2)}) async-start(), calls=%async_computation.1 | async-start | bytes 13369344 | tf_op jit(solution)/shard_map/all_gather | solution.py:49
  9.5 9.6 %copy-start.1 = (bf16[16,4,2048]{2,1,0:T(4,128)(2,1)S(1)}, bf16[16,4,2048]{2,1,0:T(4,128)(2,1)}, u32[]{:S(2)}) copy-start(bf16[16,4,2048]{2,1,0:T(4,128)(2,1)} %param.6) | copy-start | bytes 786436
  39.7 217.6 %all-gather.5.cloned.1.call-start = ((), (), s32[]{:S(2)}) async-start(), calls=%async_computation.2 | async-start | bytes 1671168 | tf_op jit(solution)/shard_map/all_gather | solution.py:46
  40.5 493.8 %all-reduce.4.cloned.1.call-start = ((), (), s32[]{:S(2)}) async-start(), calls=%async_computation.3 | async-start | bytes 393216 | tf_op jit(solution)/shard_map/psum | solution.py:56
  40.9 5.7 collective-permute-start
  45.0 7.5 %collective-permute-start.1 = (f32[192,1,128]{2,1,0:T(1,128)S(1)}, f32[192,1,128]{2,1,0:T(1,128)S(1)}, u32[]{:S(2)}, u32[]{:S(2)}) collective-permute-start(f32[192,1,128]{2,1,0:T(1,128)S(1)} %get-tuple-element.7), channel_id=1, source_target_pairs={{16,0},{32,16},{48,32},{64,48},{80,64},{96,80},{112,96},{128,112},... | collective-permute-start | bytes 294920 | tf_op jit(solution)/shard_map/ppermute | solution.py:20
  53.9 5.4 collective-permute-start.2
  57.7 8.6 %collective-permute-start.3 = (f32[192,1,128]{2,1,0:T(1,128)S(1)}, f32[192,1,128]{2,1,0:T(1,128)S(1)}, u32[]{:S(2)}, u32[]{:S(2)}) collective-permute-start(f32[192,1,128]{2,1,0:T(1,128)S(1)} %get-tuple-element.5), channel_id=1, source_target_pairs={{16,0},{32,16},{48,32},{64,48},{80,64},{96,80},{112,96},{128,112},... | collective-permute-start | bytes 294920 | tf_op jit(solution)/shard_map/ppermute | solution.py:20
  206.5 327.8 %copy-start.3 = (bf16[192,256]{1,0:T(8,128)(2,1)S(1)}, bf16[192,256]{1,0:T(8,128)(2,1)}, u32[]{:S(2)}) copy-start(bf16[192,256]{1,0:T(8,128)(2,1)} %param.11) | copy-start | bytes 294916
  261.4 392.2 %reduce-scatter.2.cloned.1.call-start = ((), (), s32[]{:S(2)}) async-start(), calls=%async_computation.4 | async-start | bytes 2228224 | tf_op jit(solution)/shard_map/reduce_scatter | solution.py:58
  535.2 1.9 copy-start.2
Sparse Core Ops, SparseCore 0:
  39.8 156.4 all-gather.2
  199.5 57.7 all-gather.4
  261.5 272.7 all-reduce.3
  539.7 113.8 reduce-scatter.1
where the time goes:
time: 662 us
  waiting for transfers between devices  583 us (88%)
  local copies, waits for them, and re-layouts  20.7 us (3%)
  other arithmetic  17.5 us (3%)
  matrix products  16.1 us (2%)
  between operations  13.9 us (2%)
  starting transfers between devices  10.8 us (2%)
    psum x1, waiting for transfers between devices, per_device(): gram_prod = lax.psum(partial_value, 'mp') / (cells_here * slab_count)  273 us
    all_gather x1, waiting for transfers between devices, per_device(): lax.all_gather(sens, 'dp', axis=0, tiled=True)  129 us
    reduce_scatter x1, waiting for transfers between devices, per_device(): lax.psum_scatter(lax.dot_general(smooth, data_update, (((0,), (0,)), ((),...  116 us
    all_gather x1, waiting for transfers between devices, per_device(): residual_whole = lax.all_gather(residual_cols, 'dp', axis=0, tiled=True)  50.8 us
  transfers between devices with their start and end apart: 8, of which 8 were waited for; matrix products, arithmetic and copies ran while one was open for 2% of the time, Pallas kernels for 0%

commit v1 on v0

v1 whole, which is shorter than its diff:
```python
import functools
import math

import jax
import jax.numpy as jnp
from jax import lax
from jax.experimental import pallas as pl
from jax.experimental.pallas import tpu as pltpu
from jax.sharding import PartitionSpec as P

BF, F32 = jnp.bfloat16, jnp.float32
COLS = 128
HALO = 2 * COLS
NREC, NFREQ, KC = 64, 16, 4
FK, RK = NFREQ * KC, NREC * KC
DATA, RHS, BLOCKS, SLABS = 192, 256, 16, 32
NDATA, CELLS = DATA * BLOCKS, 2048
Q = RHS // BLOCKS
TILES = NDATA // 128
GRID_ROWS = CELLS // COLS
NT = (((1,), (1,)), ((), ()))


def whole(n):
    return [pl.BlockSpec(memory_space=pltpu.VMEM)] * n


def pack_kernel(res_ref, coef_ref, rec_ref, freq_ref, out_ref, big, small):
    odd = lax.rem(lax.axis_index("dp"), 2) == 1
    big[...] = jnp.zeros_like(big)
    small[...] = jnp.zeros_like(small)
    big[0:DATA, :] = res_ref[...].astype(F32)
    small[0:DATA, 0:KC] = coef_ref[...]
    res = jnp.transpose(big[...])
    coef = jnp.transpose(small[...])[0:8]
    hi = coef.astype(BF).astype(F32)
    lo = coef - hi
    pad = jnp.zeros((1, 64), F32)
    rec = jnp.concatenate([rec_ref[...].astype(F32), pad], axis=1)
    freq = jnp.concatenate([freq_ref[...].astype(F32), pad], axis=1)
    row = lax.broadcasted_iota(jnp.int32, (8, 256), 0)
    head = jnp.where(row < KC, hi, pltpu.roll(lo, KC, 0))
    index = jnp.where(row == 0, rec, jnp.where(row == 1, freq, 0.0))
    side = jnp.concatenate([head, index], axis=0)

    def place(v):
        tail = v[:, 128:256]
        tail = jnp.where(odd, pltpu.roll(tail, 64, 1), tail)
        return jnp.concatenate([v[:, 0:128], tail], axis=1).astype(BF)

    res = place(res)
    side = place(side)
    for b in range(BLOCKS):
        out_ref[b, 0:Q, :] = res[b * Q : (b + 1) * Q]
        out_ref[b, Q : 2 * Q, :] = side


def tile_of(recv_ref, t, lo):
    if t < BLOCKS:
        return recv_ref[t, lo : lo + 16, 0:128].astype(F32)
    p = 2 * (t - BLOCKS)
    return recv_ref[p, lo : lo + 16, 128:256].astype(F32) + recv_ref[p + 1, lo : lo + 16, 128:256].astype(F32)


def data_side(recv_ref, weight, onehot):
    sub = lax.broadcasted_iota(jnp.int32, (8, 128), 0) // KC
    row = (lax.broadcasted_iota(jnp.int32, (RK, 128), 0) // KC).astype(F32)
    for t in range(TILES):
        at = slice(t * 128, (t + 1) * 128)
        side = tile_of(recv_ref, t, Q)
        coef = 0.5 * (side[0:8] + pltpu.roll(side[0:8], KC, 0))
        rec, freq = side[8:9], side[9:10]
        for g in range(FK // 8):
            weight[g * 8 : g * 8 + 8, at] = jnp.where(freq == (sub + 2 * g).astype(F32), coef, 0.0)
        onehot[:, at] = jnp.where(rec == row, 1.0, 0.0).astype(BF)


def expand(weight, x_ref, basis, z, acc, v, n, width):
    acc[...] = jnp.zeros_like(acc)

    def step(i, _):
        at = pl.ds(pl.multiple_of(i * width, width), width)
        x = x_ref[:, at]
        for fk in range(FK):
            z[fk * Q : (fk + 1) * Q, :] = (weight[fk : fk + 1, at] * x).astype(BF)
        acc[...] += lax.dot_general(z[...], basis[:, at], NT, preferred_element_type=F32)
        return 0

    lax.fori_loop(0, n // width, step, 0)
    shape = (FK * Q, RK)
    k_row = lax.rem(lax.broadcasted_iota(jnp.int32, shape, 0) // Q, KC)
    k_col = lax.rem(lax.broadcasted_iota(jnp.int32, shape, 1), KC)
    v[...] = jnp.where(k_row == k_col, acc[...], 0.0).astype(BF)


def contract_tile(v, basis, weight):
    u = jnp.dot(v, basis, preferred_element_type=F32)
    total = [jnp.zeros((Q, u.shape[1]), F32) for _ in range(4)]
    for fk in range(FK):
        total[fk % 4] = total[fk % 4] + weight(fk) * u[fk * Q : (fk + 1) * Q, :]
    return (total[0] + total[1]) + (total[2] + total[3])


def smooth_rows(rows, first, last):
    lane = lax.broadcasted_iota(jnp.int32, (Q, COLS), 1)

    def sweep(rows):
        out = []
        for i in range(1, len(rows) - 1):
            x = rows[i]
            left = jnp.where(lane == 0, 0.0, pltpu.roll(x, 1, 1))
            right = jnp.where(lane == COLS - 1, 0.0, pltpu.roll(x, COLS - 1, 1))
            out.append(x + 0.2 * ((rows[i - 1] + rows[i + 1] + left + right) - 4.0 * x))
        return out

    once = sweep(rows)
    once[0] = once[0] * jnp.where(first, 0.0, 1.0)
    once[-1] = once[-1] * jnp.where(last, 0.0, 1.0)
    return sweep(once)


def cells_from_data(v, adj_ref, up_ref, down_ref, field, cell):
    def step(i, _):
        at = pl.ds(pl.multiple_of(i * 256, 256), 256)
        cell[:, at] = contract_tile(v[...], adj_ref[:, at], lambda fk: field[fk : fk + 1, at])
        return 0

    lax.fori_loop(0, CELLS // 256, step, 0)
    edges = []
    for i, edge in enumerate((up_ref, down_ref)):
        at = slice(CELLS + i * HALO, CELLS + (i + 1) * HALO)
        edges.append(contract_tile(v[...], edge[0:RK, :], lambda fk: field[fk : fk + 1, at]))
    up, down = edges
    rows = [up[:, 0:COLS], up[:, COLS:]]
    rows += [cell[:, r * COLS : (r + 1) * COLS] for r in range(GRID_ROWS)]
    rows += [down[:, 0:COLS], down[:, COLS:]]
    j = lax.axis_index("mp")
    return smooth_rows(rows, j == 0, j == SLABS - 1)


def load_fields(fwd_ref, up_ref, down_ref, field):
    field[:, 0:CELLS] = fwd_ref[...].astype(F32)
    field[:, CELLS : CELLS + HALO] = up_ref[RK:, :].astype(F32)
    field[:, CELLS + HALO :] = down_ref[RK:, :].astype(F32)


def gram_kernel(recv_ref, adj_ref, fwd_ref, up_ref, down_ref, gram_ref, tiles_ref, weight, onehot, field, x, cell, z, acc, v):
    load_fields(fwd_ref, up_ref, down_ref, field)
    data_side(recv_ref, weight, onehot)
    for t in range(TILES):
        tile = tile_of(recv_ref, t, 0)
        x[:, t * 128 : (t + 1) * 128] = tile
        tiles_ref[t] = tile
    for t in range(TILES, SLABS):
        tiles_ref[t] = jnp.zeros((Q, 128), F32)
        gram_ref[t] = jnp.zeros((Q, 128), F32)
    expand(weight, x, onehot, z, acc, v, NDATA, 512)
    rows = cells_from_data(v, adj_ref, up_ref, down_ref, field, cell)
    for r in range(GRID_ROWS):
        cell[:, r * COLS : (r + 1) * COLS] = rows[r] * (1.0 / (CELLS * SLABS))
    expand(field, cell, adj_ref, z, acc, v, CELLS, 512)

    def step(i, _):
        at = pl.ds(pl.multiple_of(i * 256, 256), 256)
        g = contract_tile(v[...], onehot[:, at], lambda fk: weight[fk : fk + 1, at])
        gram_ref[2 * i] = g[:, 0:128]
        gram_ref[2 * i + 1] = g[:, 128:256]
        return 0

    lax.fori_loop(0, TILES // 2, step, 0)


def update_kernel(parts_ref, tiles_ref, out_ref):
    total = tiles_ref[lax.axis_index("mp")]
    for j in range(SLABS):
        total = total + parts_ref[j]
    total = total.astype(BF)
    for j in range(SLABS):
        out_ref[j] = total


def model_kernel(recv_ref, upd_ref, adj_ref, fwd_ref, up_ref, down_ref, out_ref, weight, onehot, field, x, cell, z, acc, v):
    load_fields(fwd_ref, up_ref, down_ref, field)
    data_side(recv_ref, weight, onehot)
    for t in range(TILES):
        x[:, t * 128 : (t + 1) * 128] = upd_ref[t].astype(F32)
    expand(weight, x, onehot, z, acc, v, NDATA, 512)
    rows = cells_from_data(v, adj_ref, up_ref, down_ref, field, cell)
    for b in range(BLOCKS):
        out_ref[b, 0:Q, :] = (rows[b] * (1.0 / math.sqrt(NDATA))).astype(BF)
        out_ref[b, Q : 2 * Q, :] = upd_ref[b]
        out_ref[b, 2 * Q : 3 * Q, :] = upd_ref[BLOCKS + b // 2]


def finish_kernel(recv_ref, upd_ref, model_ref):
    odd = lax.rem(lax.axis_index("dp"), 2) == 1
    part = lambda i: jnp.concatenate([recv_ref[b, i * Q : (i + 1) * Q, :] for b in range(BLOCKS)], axis=0).astype(F32)
    model_ref[...] = jnp.transpose(part(0))
    upd_ref[0:128, :] = jnp.transpose(part(1)).astype(BF)
    tail = part(2)
    tail = jnp.where(odd, pltpu.roll(tail, 64, 1), tail)
    upd_ref[128:DATA, :] = jnp.transpose(tail)[0:64].astype(BF)


def per_device(forward_fields, adjoint_fields, data_rec, data_freq, data_coef, residual_cols):
    shape = jax.ShapeDtypeStruct
    params = pltpu.CompilerParams(vmem_limit_bytes=40 * 1024 * 1024)
    call = functools.partial(pl.pallas_call, compiler_params=params)
    adj = adjoint_fields.reshape(RK, CELLS)
    fwd = forward_fields.reshape(FK, CELLS)
    send_down = jnp.concatenate([adj[:, -HALO:], fwd[:, -HALO:]], axis=0)
    send_up = jnp.concatenate([adj[:, :HALO], fwd[:, :HALO]], axis=0)
    to_next = [(i, i + 1) for i in range(SLABS - 1)]
    up = lax.ppermute(send_down, "mp", to_next)
    down = lax.ppermute(send_up, "mp", [(b, a) for a, b in to_next])
    packed = call(
        pack_kernel,
        out_shape=shape((BLOCKS, 2 * Q, 256), BF),
        in_specs=whole(4),
        out_specs=whole(1)[0],
        scratch_shapes=[pltpu.VMEM((256, RHS), F32), pltpu.VMEM((256, 128), F32)],
    )(residual_cols, data_coef, data_rec.reshape(1, DATA), data_freq.reshape(1, DATA))
    recv = lax.all_to_all(packed, "dp", 0, 0)
    scratch = [
        pltpu.VMEM((FK, NDATA), F32),
        pltpu.VMEM((RK, NDATA), BF),
        pltpu.VMEM((FK, CELLS + 2 * HALO), F32),
        pltpu.VMEM((Q, NDATA), F32),
        pltpu.VMEM((Q, CELLS), F32),
        pltpu.VMEM((FK * Q, 512), BF),
        pltpu.VMEM((FK * Q, RK), F32),
        pltpu.VMEM((FK * Q, RK), BF),
    ]
    gram, tiles = call(
        gram_kernel,
        out_shape=[shape((SLABS, Q, 128), F32), shape((SLABS, Q, 128), F32)],
        in_specs=whole(5),
        out_specs=whole(2),
        scratch_shapes=scratch,
    )(recv, adj, fwd, up, down)
    parts = lax.all_to_all(gram, "mp", 0, 0)
    mine = call(update_kernel, out_shape=shape((SLABS, Q, 128), BF), in_specs=whole(2), out_specs=whole(1)[0])(parts, tiles)
    update = lax.all_to_all(mine, "mp", 0, 0)
    rows = call(
        model_kernel,
        out_shape=shape((BLOCKS, 3 * Q, 128), BF),
        in_specs=whole(6),
        out_specs=whole(1)[0],
        scratch_shapes=scratch,
    )(recv, update, adj, fwd, up, down)
    last = lax.all_to_all(rows, "dp", 0, 0)
    return call(
        finish_kernel,
        out_shape=[shape((DATA, RHS), BF), shape((COLS, RHS), F32)],
        in_specs=whole(1),
        out_specs=whole(2),
    )(last)


def solution(mesh):
    in_specs = (
        P(None, None, "mp"),
        P(None, None, "mp"),
        P("dp"),
        P("dp"),
        P("dp", None),
        P("dp", None),
    )
    out_specs = (P("dp", None), P(("mp", "dp"), None))
    return jax.shard_map(
        per_device, mesh=mesh, in_specs=in_specs, out_specs=out_specs, check_vma=False
    )
```

time: 662 us -> 111 us (0.17)
  waiting for transfers between devices: 583 us -> 6.55 us
  blocking collectives: 0 us -> 63.7 us
  Pallas kernels: 0 us -> 21.7 us
  local copies, waits for them, and re-layouts: 20.7 us -> 2.84 us
  other arithmetic: 17.5 us -> 0.03 us
  matrix products: 16.1 us -> 0 us
  between operations: 13.9 us -> 0.75 us
    psum x1 -> x0, waiting for transfers between devices: 273 us -> none  [per_device(): gram_prod = lax.psum(partial_value, 'mp') / (cells_here * slab_count)]
    all_gather x2 -> x0, waiting for transfers between devices: 179 us -> none  [the longest x1 129 us: per_device(): lax.all_gather(sens, 'dp', axis=0, tiled=True)]
    reduce_scatter x1 -> x0, waiting for transfers between devices: 116 us -> none  [per_device(): lax.psum_scatter(lax.dot_general(smooth, data_update, (((0,), (0,)), ((),...]
    all_to_all x0 -> x3, blocking collectives: none -> 63.7 us  [the longest x1 28 us: per_device(): parts = lax.all_to_all(gram, 'mp', 0, 0)]
    pallas_call x0 -> x5, Pallas kernels: none -> 21.7 us  [the longest x1 13 us: per_device(): call(gram_kernel, out_shape=[shape((SLABS, Q, 128), F32), shape((SLABS, Q...]
    gather x2 -> x0, local copies, waits for them, and re-layouts: 19.3 us -> none  [the longest x1 9.69 us: per_device(): forward = forward_fields[data_freq].astype(jnp.float32)]
    dot_general x3 -> x0, matrix products: 16.1 us -> none  [the longest x1 10.2 us: per_device(): lax.dot_general(smooth, lax.all_gather(sens, 'dp', axis=0, tiled=True), (...]
    all_to_all x0 -> x1, starting transfers between devices: none -> 11.1 us  [per_device(): recv = lax.all_to_all(packed, 'dp', 0, 0)]
  transfers between devices with their start and end apart: 8 -> 3, of which waited for: 8 -> 2; matrix products, arithmetic and copies ran while one was open for 2% -> 1% of each run, Pallas kernels for 0% -> 0%
where the time goes in v1:
time: 111 us; the launch traced here: 110 us
  blocking collectives  63.7 us (57%)
  Pallas kernels  21.7 us (20%)
  starting transfers between devices  14.7 us (13%)
  waiting for transfers between devices  6.55 us (6%)
  local copies, waits for them, and re-layouts  2.84 us (3%)
    all_to_all x1, blocking collectives, per_device(): parts = lax.all_to_all(gram, 'mp', 0, 0)  28 us
    all_to_all x1, blocking collectives, per_device(): last = lax.all_to_all(rows, 'dp', 0, 0)  20.6 us
    all_to_all x1, blocking collectives, per_device(): update = lax.all_to_all(mine, 'mp', 0, 0)  15.1 us
    pallas_call x1, Pallas kernels, per_device(): call(gram_kernel, out_shape=[shape((SLABS, Q, 128), F32), shape((SLABS, Q...  13 us
    all_to_all x1, starting transfers between devices, per_device(): recv = lax.all_to_all(packed, 'dp', 0, 0)  11.1 us
    pallas_call x1, Pallas kernels, per_device(): call(model_kernel, out_shape=shape((BLOCKS, 3 * Q, 128), BF), in_specs=wh...  6.84 us
    ppermute x1, waiting for transfers between devices, per_device(): up = lax.ppermute(send_down, 'mp', to_next)  5.06 us
    ppermute x1, starting transfers between devices, per_device(): up = lax.ppermute(send_down, 'mp', to_next)  2.33 us
  transfers between devices with their start and end apart: 3, of which 2 were waited for; matrix products, arithmetic and copies ran while one was open for 1% of the time, Pallas kernels for 0%

profile of v1, /device:TPU:1, one launch (start us, length us, event | category | flops | bytes accessed | tf_op | source)
XLA Modules:
  0.0 110.3 jit_solution(3196824698330305295)
XLA Ops:
  0.6 0.0 copy-start
  0.6 0.8 copy.8.coef_ref
  1.5 0.0 copy-start.2
  1.5 0.0 copy-start.1
  1.5 0.0 copy-start.3
  1.5 0.0 copy-done
  1.5 0.6 copy-done.2
  2.2 0.0 copy-done.1
  2.2 0.9 shard_map.77
  3.1 11.1 %all-to-all-start = ((bf16[16,32,256]{2,1,0:T(8,128)(2,1)}), bf16[16,32,256]{2,1,0:T(8,128)(2,1)S(1)}, u32[]{:S(2)}, u32[]{:S(2)}) async-start(bf16[16,32,256]{2,1,0:T(8,128)(2,1)} %shard_map.77), calls=%async_computation | async-start | bytes 524288 | tf_op jit(solution)/shard_map/all_to_all | solution.py:223
  14.2 1.0 reshape.19.fwd_ref
  15.2 0.0 copy-done.3
  15.2 0.3 reshape.18.adj_ref
  15.5 2.3 %collective-permute-start = (bf16[320,256]{1,0:T(8,128)(2,1)S(1)}, bf16[320,256]{1,0:T(8,128)(2,1)S(1)}, u32[]{:S(2)}, u32[]{:S(2)}) collective-permute-start(bf16[320,256]{1,0:T(8,128)(2,1)S(1)} %pad_maximum_fusion), channel_id=1, source_target_pairs={{0,16},{16,32},{32,48},{48,64},{64,80},{80,96},{96,112},{112,128},... | collective-permute-start | bytes 491528 | tf_op jit(solution)/shard_map/ppermute | solution.py:214
  17.9 1.3 %collective-permute-start.1 = (bf16[320,256]{1,0:T(8,128)(2,1)S(1)}, bf16[320,256]{1,0:T(8,128)(2,1)S(1)}, u32[]{:S(2)}, u32[]{:S(2)}) collective-permute-start(bf16[320,256]{1,0:T(8,128)(2,1)S(1)} %pad_maximum_fusion.1), channel_id=1, source_target_pairs={{16,0},{32,16},{48,32},{64,48},{80,64},{96,80},{112,96},{128,112},... | collective-permute-start | bytes 491528 | tf_op jit(solution)/shard_map/ppermute | solution.py:215
  19.2 5.1 %collective-permute-done.up_ref = bf16[320,256]{1,0:T(8,128)(2,1)S(1)} collective-permute-done((bf16[320,256]{1,0:T(8,128)(2,1)S(1)}, bf16[320,256]{1,0:T(8,128)(2,1)S(1)}, u32[]{:S(2)}, u32[]{:S(2)}) %collective-permute-start) | collective-permute-done | bytes 163872 | tf_op jit(solution)/shard_map/ppermute | solution.py:214
  24.3 1.5 %collective-permute-done.1.down_ref = bf16[320,256]{1,0:T(8,128)(2,1)S(1)} collective-permute-done((bf16[320,256]{1,0:T(8,128)(2,1)S(1)}, bf16[320,256]{1,0:T(8,128)(2,1)S(1)}, u32[]{:S(2)}, u32[]{:S(2)}) %collective-permute-start.1) | collective-permute-done | bytes 163872 | tf_op jit(solution)/shard_map/ppermute | solution.py:215
  25.8 0.0 all-to-all-done.recv_ref
  25.8 13.0 %shard_map.78 = (f32[32,16,128]{2,1,0:T(8,128)S(1)}, f32[32,16,128]{2,1,0:T(8,128)S(1)}) custom-call(bf16[16,32,256]{2,1,0:T(8,128)(2,1)S(1)} %all-to-all-done.recv_ref, bf16[256,2048]{1,0:T(8,128)(2,1)S(1)} %reshape.18.adj_ref, bf16[64,2048]{1,0:T(8,128)(2,1)S(1)} %reshape.19.fwd_ref, bf16[320,256]{1,0:T(8,128)(2,1)S(1)} %collective-permute-done.up_ref, ...), custom_call_target="tpu_custom_call" | custom-call | tf_op jit(solution)/shard_map/pallas_call | solution.py:234
  38.8 28.0 %all_to_all.20.parts_ref = f32[32,16,128]{2,1,0:T(8,128)S(1)} all-to-all(f32[32,16,128]{2,1,0:T(8,128)S(1)} %get-tuple-element.4), channel_id=1, replica_groups=mesh['mp'=32,'dp'=16] {'mp'}, dimensions={0} | all-to-all | bytes 524288 | tf_op jit(solution)/shard_map/all_to_all | solution.py:241
  66.8 0.1 shard_map.79
  66.9 15.1 %all_to_all.21.upd_ref = bf16[32,16,128]{2,1,0:T(8,128)(2,1)S(1)} all-to-all(bf16[32,16,128]{2,1,0:T(8,128)(2,1)S(1)} %shard_map.79), channel_id=1, replica_groups=mesh['mp'=32,'dp'=16] {'mp'}, dimensions={0} | all-to-all | bytes 262144 | tf_op jit(solution)/shard_map/all_to_all | solution.py:243
  82.0 6.8 %shard_map.80 = bf16[16,48,128]{2,1,0:T(8,128)(2,1)S(1)} custom-call(bf16[16,32,256]{2,1,0:T(8,128)(2,1)S(1)} %all-to-all-done.recv_ref, bf16[32,16,128]{2,1,0:T(8,128)(2,1)S(1)} %all_to_all.21.upd_ref, bf16[256,2048]{1,0:T(8,128)(2,1)S(1)} %reshape.18.adj_ref, bf16[64,2048]{1,0:T(8,128)(2,1)S(1)} %reshape.19.fwd_ref, ...), custom_call_target="tpu_custom_call" | custom-call | tf_op jit(solution)/shard_map/pallas_call | solution.py:244
  88.8 20.6 %all_to_all.22.recv_ref = bf16[16,48,128]{2,1,0:T(8,128)(2,1)S(1)} all-to-all(bf16[16,48,128]{2,1,0:T(8,128)(2,1)S(1)} %shard_map.80), channel_id=1, replica_groups=mesh['mp'=32,'dp'=16] {'dp'}, dimensions={0} | all-to-all | bytes 393216 | tf_op jit(solution)/shard_map/all_to_all | solution.py:251
  109.4 0.9 shard_map.81
  (4 shorter events, 0.1 us)
Async XLA Ops:
  0.6 0.9 copy-start
  1.5 0.7 copy-start.2
  1.5 0.7 copy-start.1
  1.5 13.7 %copy-start.3 = (bf16[64,4,2048]{2,1,0:T(4,128)(2,1)S(1)}, bf16[64,4,2048]{2,1,0:T(4,128)(2,1)}, u32[]{:S(2)}) copy-start(bf16[64,4,2048]{2,1,0:T(4,128)(2,1)} %param.7) | copy-start | bytes 3145732
  3.1 22.7 %all-to-all-start = ((bf16[16,32,256]{2,1,0:T(8,128)(2,1)}), bf16[16,32,256]{2,1,0:T(8,128)(2,1)S(1)}, u32[]{:S(2)}, u32[]{:S(2)}) async-start(bf16[16,32,256]{2,1,0:T(8,128)(2,1)} %shard_map.77), calls=%async_computation | async-start | bytes 524288 | tf_op jit(solution)/shard_map/all_to_all | solution.py:223
  15.5 8.7 %collective-permute-start = (bf16[320,256]{1,0:T(8,128)(2,1)S(1)}, bf16[320,256]{1,0:T(8,128)(2,1)S(1)}, u32[]{:S(2)}, u32[]{:S(2)}) collective-permute-start(bf16[320,256]{1,0:T(8,128)(2,1)S(1)} %pad_maximum_fusion), channel_id=1, source_target_pairs={{0,16},{16,32},{32,48},{48,64},{64,80},{80,96},{96,112},{112,128},... | collective-permute-start | bytes 491528 | tf_op jit(solution)/shard_map/ppermute | solution.py:214
  17.9 7.8 %collective-permute-start.1 = (bf16[320,256]{1,0:T(8,128)(2,1)S(1)}, bf16[320,256]{1,0:T(8,128)(2,1)S(1)}, u32[]{:S(2)}, u32[]{:S(2)}) collective-permute-start(bf16[320,256]{1,0:T(8,128)(2,1)S(1)} %pad_maximum_fusion.1), channel_id=1, source_target_pairs={{16,0},{32,16},{48,32},{64,48},{80,64},{96,80},{112,96},{128,112},... | collective-permute-start | bytes 491528 | tf_op jit(solution)/shard_map/ppermute | solution.py:215

commit v2 on v1

v2 whole, which is shorter than its diff:
```python
import functools
import math

import jax
import jax.numpy as jnp
from jax import lax
from jax.experimental import pallas as pl
from jax.experimental.pallas import tpu as pltpu
from jax.sharding import PartitionSpec as P

BF, F32 = jnp.bfloat16, jnp.float32
COLS = 128
HALO = 2 * COLS
NREC, NFREQ, KC = 64, 16, 4
FK, RK = NFREQ * KC, NREC * KC
DATA, RHS, BLOCKS, SLABS = 192, 256, 16, 32
NDATA, CELLS = DATA * BLOCKS, 2048
Q = RHS // BLOCKS
TILES = NDATA // 128
GRID_ROWS = CELLS // COLS
NT = (((1,), (1,)), ((), ()))


NEAR = [
    [(j if i & 2 == 0 else j ^ 2) * BLOCKS + i for i in range(BLOCKS)] for j in range(SLABS)
]


def whole(n):
    return [pl.BlockSpec(memory_space=pltpu.VMEM)] * n


def pack_kernel(res_ref, coef_ref, rec_ref, freq_ref, out_ref, big, side):
    odd = lax.rem(lax.axis_index("dp"), 2) == 1
    big[...] = jnp.zeros_like(big)
    side[...] = jnp.zeros_like(side)
    big[0:DATA, :] = res_ref[...].astype(F32)
    coef = coef_ref[...]
    hi = coef.astype(BF).astype(F32)
    side[0:KC, 0:DATA] = hi
    side[KC : 2 * KC, 0:DATA] = coef - hi
    side[8:9, 0:DATA] = rec_ref[...].astype(F32)
    side[9:10, 0:DATA] = freq_ref[...].astype(F32)

    def place(v):
        tail = v[:, 128:256]
        tail = jnp.where(odd, pltpu.roll(tail, 64, 1), tail)
        return jnp.concatenate([v[:, 0:128], tail], axis=1).astype(BF)

    res = place(jnp.transpose(big[...]))
    rest = place(side[...])
    for b in range(BLOCKS):
        out_ref[b, 0:Q, :] = res[b * Q : (b + 1) * Q]
        out_ref[b, Q : 2 * Q, :] = rest


def tile_of(recv_ref, t, lo):
    if t < BLOCKS:
        return recv_ref[t, lo : lo + 16, 0:128].astype(F32)
    p = 2 * (t - BLOCKS)
    return recv_ref[p, lo : lo + 16, 128:256].astype(F32) + recv_ref[p + 1, lo : lo + 16, 128:256].astype(F32)


def pick_data(recv_ref, pick, freqs):
    sub = lax.broadcasted_iota(jnp.int32, (8, 128), 0) // KC
    for t in range(TILES):
        at = slice(t * 128, (t + 1) * 128)
        side = tile_of(recv_ref, t, Q)
        coef = 0.5 * (side[0:8] + pltpu.roll(side[0:8], KC, 0))
        rec = side[8:9]
        freqs[:, at] = jnp.broadcast_to(side[9:10], (8, 128))
        for g in range(RK // 16):
            two = [jnp.where(rec == (sub + 2 * (2 * g + i)).astype(F32), coef, 0.0) for i in range(2)]
            pick[g * 16 : g * 16 + 16, at] = jnp.concatenate(two, axis=0).astype(BF)


def of_component(v, k):
    lane = lax.rem(lax.broadcasted_iota(jnp.int32, v.shape, 1), KC)
    return jnp.where(lane == k, v, 0.0)


def from_data(tiles, pick, freqs, z, v):
    for t in range(TILES):
        at = slice(t * 128, (t + 1) * 128)
        x = tiles(t)
        freq = jnp.concatenate([freqs[:, at], freqs[:, at]], axis=0)
        for f in range(NFREQ):
            z[f * Q : (f + 1) * Q, at] = jnp.where(freq == float(f), x, 0.0).astype(BF)
    w = lax.dot_general(z[...], pick[...], NT, preferred_element_type=F32)
    for f in range(NFREQ):
        for k in range(KC):
            fk = f * KC + k
            v[fk * Q : (fk + 1) * Q, :] = of_component(w[f * Q : (f + 1) * Q], k).astype(BF)


def to_cells(v, basis, field):
    u = jnp.dot(v[...], basis, preferred_element_type=F32)
    total = [jnp.zeros((Q, u.shape[1]), F32) for _ in range(4)]
    for fk in range(FK):
        total[fk % 4] = total[fk % 4] + field(fk) * u[fk * Q : (fk + 1) * Q, :]
    return (total[0] + total[1]) + (total[2] + total[3])


def center_cells(v, adj_ref, field, cell):
    for i in range(CELLS // 256):
        at = slice(i * 256, (i + 1) * 256)
        cell[:, at] = to_cells(v, adj_ref[:, at], lambda fk: field[fk : fk + 1, at])


def with_edges(v, up_ref, down_ref, edge, cell):
    edge[:, 0:HALO] = up_ref[RK:, :].astype(F32)
    edge[:, HALO:] = down_ref[RK:, :].astype(F32)
    up = to_cells(v, up_ref[0:RK, :], lambda fk: edge[fk : fk + 1, 0:HALO])
    down = to_cells(v, down_ref[0:RK, :], lambda fk: edge[fk : fk + 1, HALO:])
    rows = [up[:, 0:COLS], up[:, COLS:]]
    rows += [cell[:, r * COLS : (r + 1) * COLS] for r in range(GRID_ROWS)]
    rows += [down[:, 0:COLS], down[:, COLS:]]
    j = lax.axis_index("mp")
    return smooth_rows(rows, j == 0, j == SLABS - 1)


def back_kernel(recv_ref, adj_ref, fwd_ref, pick, freqs, tiles_ref, v, field, cell, z):
    field[...] = fwd_ref[...].astype(F32)
    pick_data(recv_ref, pick, freqs)
    for t in range(TILES):
        tiles_ref[t] = tile_of(recv_ref, t, 0)
    for t in range(TILES, SLABS):
        tiles_ref[t] = jnp.zeros((Q, 128), F32)
    from_data(lambda t: tiles_ref[t], pick, freqs, z, v)
    center_cells(v, adj_ref, field, cell)


def gram_kernel(v, cell_ref, pick, freqs, field, adj_ref, up_ref, down_ref, gram_ref, edge, z, y):
    rows = with_edges(v, up_ref, down_ref, edge, cell_ref)
    for r in range(GRID_ROWS):
        at = slice(r * COLS, (r + 1) * COLS)
        x = rows[r] * (1.0 / (CELLS * SLABS))
        for fk in range(FK):
            z[fk * Q : (fk + 1) * Q, at] = (field[fk : fk + 1, at] * x).astype(BF)
    w = lax.dot_general(z[...], adj_ref[...], NT, preferred_element_type=F32)
    for f in range(NFREQ):
        part = [of_component(w[(f * KC + k) * Q : (f * KC + k + 1) * Q], k) for k in range(KC)]
        y[f * Q : (f + 1) * Q, :] = ((part[0] + part[1]) + (part[2] + part[3])).astype(BF)
    for i in range(TILES // 2):
        at = slice(i * 256, (i + 1) * 256)
        u = jnp.dot(y[...], pick[:, at], preferred_element_type=F32)
        freq = jnp.concatenate([freqs[:, at], freqs[:, at]], axis=0)
        g = jnp.zeros((Q, 256), F32)
        for f in range(NFREQ):
            g = jnp.where(freq == float(f), u[f * Q : (f + 1) * Q], g)
        gram_ref[2 * i] = g[:, 0:128]
        gram_ref[2 * i + 1] = g[:, 128:256]
    for t in range(TILES, SLABS):
        gram_ref[t] = jnp.zeros((Q, 128), F32)


def smooth_rows(rows, first, last):
    lane = lax.broadcasted_iota(jnp.int32, (Q, COLS), 1)

    def sweep(rows):
        out = []
        for i in range(1, len(rows) - 1):
            x = rows[i]
            left = jnp.where(lane == 0, 0.0, pltpu.roll(x, 1, 1))
            right = jnp.where(lane == COLS - 1, 0.0, pltpu.roll(x, COLS - 1, 1))
            out.append(x + 0.2 * ((rows[i - 1] + rows[i + 1] + left + right) - 4.0 * x))
        return out

    once = sweep(rows)
    once[0] = once[0] * jnp.where(first, 0.0, 1.0)
    once[-1] = once[-1] * jnp.where(last, 0.0, 1.0)
    return sweep(once)


def update_kernel(parts_ref, tiles_ref, out_ref):
    total = tiles_ref[lax.axis_index("mp")]
    for j in range(SLABS):
        total = total + parts_ref[j]
    total = total.astype(BF)
    for j in range(SLABS):
        out_ref[j] = total


def model_kernel(upd_ref, pick, freqs, field, adj_ref, up_ref, down_ref, out_ref, z, v, cell, edge):
    from_data(lambda t: upd_ref[t].astype(F32), pick, freqs, z, v)
    center_cells(v, adj_ref, field, cell)
    rows = with_edges(v, up_ref, down_ref, edge, cell)
    for b in range(BLOCKS):
        out_ref[b, 0:Q, :] = (rows[b] * (1.0 / math.sqrt(NDATA))).astype(BF)
        out_ref[b, Q : 2 * Q, :] = upd_ref[b]
        out_ref[b, 2 * Q : 3 * Q, :] = upd_ref[BLOCKS + b // 2]


def finish_kernel(recv_ref, upd_ref, model_ref):
    odd = lax.rem(lax.axis_index("dp"), 2) == 1
    part = lambda i: jnp.concatenate([recv_ref[b, i * Q : (i + 1) * Q, :] for b in range(BLOCKS)], axis=0).astype(F32)
    model_ref[...] = jnp.transpose(part(0))
    upd_ref[0:128, :] = jnp.transpose(part(1)).astype(BF)
    tail = part(2)
    tail = jnp.where(odd, pltpu.roll(tail, 64, 1), tail)
    upd_ref[128:DATA, :] = jnp.transpose(tail)[0:64].astype(BF)


def per_device(forward_fields, adjoint_fields, data_rec, data_freq, data_coef, residual_cols):
    shape = jax.ShapeDtypeStruct
    params = pltpu.CompilerParams(vmem_limit_bytes=40 * 1024 * 1024)
    call = functools.partial(pl.pallas_call, compiler_params=params)
    adj = adjoint_fields.reshape(RK, CELLS)
    fwd = forward_fields.reshape(FK, CELLS)
    send_down = jnp.concatenate([adj[:, -HALO:], fwd[:, -HALO:]], axis=0)
    send_up = jnp.concatenate([adj[:, :HALO], fwd[:, :HALO]], axis=0)
    to_next = [
        (j * BLOCKS + i, (j + 1) * BLOCKS + (i ^ 2 if j % 4 == 3 else i)) for j in range(SLABS - 1) for i in range(BLOCKS)
    ]
    up = lax.ppermute(send_down, ("mp", "dp"), to_next)
    down = lax.ppermute(send_up, ("mp", "dp"), [(b, a) for a, b in to_next])
    packed = call(
        pack_kernel,
        out_shape=shape((BLOCKS, 2 * Q, 256), BF),
        in_specs=whole(4),
        out_specs=whole(1)[0],
        scratch_shapes=[pltpu.VMEM((256, RHS), F32), pltpu.VMEM((2 * KC + 8, 256), F32)],
    )(residual_cols, data_coef.T, data_rec.reshape(1, DATA), data_freq.reshape(1, DATA))
    recv = lax.all_to_all(packed, ("mp", "dp"), 0, 0, axis_index_groups=NEAR)
    pick, freqs, tiles, v, field, cell = call(
        back_kernel,
        out_shape=[
            shape((RK, NDATA), BF),
            shape((8, NDATA), F32),
            shape((SLABS, Q, 128), F32),
            shape((FK * Q, RK), BF),
            shape((FK, CELLS), F32),
            shape((Q, CELLS), F32),
        ],
        in_specs=whole(3),
        out_specs=whole(6),
        scratch_shapes=[pltpu.VMEM((NFREQ * Q, NDATA), BF)],
        cost_estimate=pl.CostEstimate(flops=4 * 10**9, bytes_accessed=8 * 10**6, transcendentals=0),
    )(recv, adj, fwd)
    gram = call(
        gram_kernel,
        out_shape=shape((SLABS, Q, 128), F32),
        in_specs=whole(8),
        out_specs=whole(1)[0],
        scratch_shapes=[
            pltpu.VMEM((FK, 2 * HALO), F32),
            pltpu.VMEM((FK * Q, CELLS), BF),
            pltpu.VMEM((NFREQ * Q, RK), BF),
        ],
    )(v, cell, pick, freqs, field, adj, up, down)
    parts = lax.all_to_all(gram, "mp", 0, 0)
    mine = call(update_kernel, out_shape=shape((SLABS, Q, 128), BF), in_specs=whole(2), out_specs=whole(1)[0])(parts, tiles)
    update = lax.all_to_all(mine, "mp", 0, 0)
    rows = call(
        model_kernel,
        out_shape=shape((BLOCKS, 3 * Q, 128), BF),
        in_specs=whole(7),
        out_specs=whole(1)[0],
        scratch_shapes=[
            pltpu.VMEM((NFREQ * Q, NDATA), BF),
            pltpu.VMEM((FK * Q, RK), BF),
            pltpu.VMEM((Q, CELLS), F32),
            pltpu.VMEM((FK, 2 * HALO), F32),
        ],
    )(update, pick, freqs, field, adj, up, down)
    last = lax.all_to_all(rows, "dp", 0, 0)
    return call(
        finish_kernel,
        out_shape=[shape((DATA, RHS), BF), shape((COLS, RHS), F32)],
        in_specs=whole(1),
        out_specs=whole(2),
    )(last)


def solution(mesh):
    in_specs = (
        P(None, None, "mp"),
        P(None, None, "mp"),
        P("dp"),
        P("dp"),
        P("dp", None),
        P("dp", None),
    )
    out_specs = (P("dp", None), P(("mp", "dp"), None))
    return jax.shard_map(
        per_device, mesh=mesh, in_specs=in_specs, out_specs=out_specs, check_vma=False
    )
```

time: 111 us -> 93.3 us (0.84)
  Pallas kernels: 21.7 us -> 10.4 us
  blocking collectives: 63.7 us -> 59.2 us
  starting transfers between devices: 14.7 us -> 13.1 us
  waiting for transfers between devices: 6.55 us -> 5.1 us
  local copies, waits for them, and re-layouts: 2.84 us -> 4.25 us
    pallas_call x1 -> x2, Pallas kernels: 13 us -> 5.62 us  [the longest x1 2.97 us: per_device(): call(gram_kernel, out_shape=shape((SLABS, Q, 128), F32), in_specs=whole(8...]
    ppermute x2, waiting for transfers between devices: 6.55 us -> 0.01 us  [the longest x1 0.01 us: per_device(): up = lax.ppermute(send_down, ('mp', 'dp'), to_next)]
    all_to_all x1, waiting for transfers between devices: 0.01 us -> 5.09 us  [per_device(): recv = lax.all_to_all(packed, ('mp', 'dp'), 0, 0, axis_index_groups=NEAR)]
    pallas_call x1, Pallas kernels: 6.84 us -> 2.97 us  [per_device(): call(model_kernel, out_shape=shape((BLOCKS, 3 * Q, 128), BF), in_specs=wh...]
    all_to_all x1, blocking collectives: 20.6 us -> 17.3 us  [per_device(): last = lax.all_to_all(rows, 'dp', 0, 0)]
    unnamed x9 -> x10, local copies, waits for them, and re-layouts: 1.52 us -> 2.93 us
  transfers between devices with their start and end apart: 3 -> 3, of which waited for: 2 -> 1; matrix products, arithmetic and copies ran while one was open for 1% -> 1% of each run, Pallas kernels for 0% -> 3%
where the time goes in v2:
time: 93.3 us; the launch traced here: 92.9 us
  blocking collectives  59.2 us (63%)
  starting transfers between devices  13.1 us (14%)
  Pallas kernels  10.4 us (11%)
  waiting for transfers between devices  5.1 us (5%)
  local copies, waits for them, and re-layouts  4.25 us (5%)
    all_to_all x1, blocking collectives, per_device(): parts = lax.all_to_all(gram, 'mp', 0, 0)  27 us
    all_to_all x1, blocking collectives, per_device(): last = lax.all_to_all(rows, 'dp', 0, 0)  17.3 us
    all_to_all x1, blocking collectives, per_device(): update = lax.all_to_all(mine, 'mp', 0, 0)  14.9 us
    all_to_all x1, starting transfers between devices, per_device(): recv = lax.all_to_all(packed, ('mp', 'dp'), 0, 0, axis_index_groups=NEAR)  10.2 us
    all_to_all x1, waiting for transfers between devices, per_device(): recv = lax.all_to_all(packed, ('mp', 'dp'), 0, 0, axis_index_groups=NEAR)  5.09 us
    pallas_call x1, Pallas kernels, per_device(): call(gram_kernel, out_shape=shape((SLABS, Q, 128), F32), in_specs=whole(8...  2.97 us
    pallas_call x1, Pallas kernels, per_device(): call(model_kernel, out_shape=shape((BLOCKS, 3 * Q, 128), BF), in_specs=wh...  2.97 us
    unnamed x10, local copies, waits for them, and re-layouts  2.93 us
  transfers between devices with their start and end apart: 3, of which 1 were waited for; matrix products, arithmetic and copies ran while one was open for 1% of the time, Pallas kernels for 3%

profile of v2, /device:TPU:1, one launch (start us, length us, event | category | flops | bytes accessed | tf_op | source)
XLA Modules:
  0.0 92.9 jit_solution(14683948938761900121)
XLA Ops:
  0.6 0.0 copy-start
  0.6 0.9 copy-done
  1.5 0.0 copy-start.1
  1.5 0.7 copy-done.1
  2.2 0.0 copy-start.2
  2.2 0.7 copy-done.2
  2.9 0.0 copy-start.3
  2.9 0.7 copy-done.3
  3.6 0.0 copy-start.4
  3.6 0.9 shard_map.77
  4.5 10.2 %all-to-all-start = ((bf16[16,32,256]{2,1,0:T(8,128)(2,1)}), bf16[16,32,256]{2,1,0:T(8,128)(2,1)S(1)}, u32[]{:S(2)}, u32[]{:S(2)}) async-start(bf16[16,32,256]{2,1,0:T(8,128)(2,1)} %shard_map.77), calls=%async_computation | async-start | bytes 524288 | tf_op jit(solution)/shard_map/all_to_all | solution.py:224
  14.7 1.0 %reshape.19.fwd_ref = bf16[64,2048]{1,0:T(8,128)(2,1)S(1)} reshape(bf16[16,4,2048]{2,1,0:T(4,128)(2,1)} %param.6) | data formatting | bytes 524288 | tf_op jit(solution)/shard_map/reshape | solution.py:209
  15.7 0.0 copy-done.4
  15.7 0.3 reshape.18.adj_ref
  16.0 1.6 %collective-permute-start = (bf16[320,256]{1,0:T(8,128)(2,1)S(1)}, bf16[320,256]{1,0:T(8,128)(2,1)S(1)}, u32[]{:S(2)}, u32[]{:S(2)}) collective-permute-start(bf16[320,256]{1,0:T(8,128)(2,1)S(1)} %pad_maximum_fusion), channel_id=1, source_target_pairs={{0,16},{1,17},{2,18},{3,19},{4,20},{5,21},{6,22},{7,23},{8,24},{9,... | collective-permute-start | bytes 491528 | tf_op jit(solution)/shard_map/ppermute | solution.py:215
  17.7 1.3 %collective-permute-start.1 = (bf16[320,256]{1,0:T(8,128)(2,1)S(1)}, bf16[320,256]{1,0:T(8,128)(2,1)S(1)}, u32[]{:S(2)}, u32[]{:S(2)}) collective-permute-start(bf16[320,256]{1,0:T(8,128)(2,1)S(1)} %pad_maximum_fusion.1), channel_id=1, source_target_pairs={{16,0},{17,1},{18,2},{19,3},{20,4},{21,5},{22,6},{23,7},{24,8},{25... | collective-permute-start | bytes 491528 | tf_op jit(solution)/shard_map/ppermute | solution.py:216
  19.0 5.1 %all-to-all-done.recv_ref = bf16[16,32,256]{2,1,0:T(8,128)(2,1)S(1)} async-done(((bf16[16,32,256]{2,1,0:T(8,128)(2,1)}), bf16[16,32,256]{2,1,0:T(8,128)(2,1)S(1)}, u32[]{:S(2)}, u32[]{:S(2)}) %all-to-all-start) | async-done | bytes 262176 | tf_op jit(solution)/shard_map/all_to_all | solution.py:224
  24.1 2.6 %shard_map.78 = (bf16[256,3072]{1,0:T(8,128)(2,1)S(1)}, f32[8,3072]{1,0:T(8,128)S(1)}, f32[32,16,128]{2,1,0:T(8,128)S(1)}, bf16[1024,256]{1,0:T(8,128)(2,1)S(1)}...) custom-call(bf16[16,32,256]{2,1,0:T(8,128)(2,1)S(1)} %all-to-all-done.recv_ref, bf16[256,2048]{1,0:T(8,128)(2,1)S(1)} %reshape.18.adj_ref, ...), custom_call_target="tpu_custom_call" | custom-call | flops 4000000000 | bytes 8000000 | tf_op jit(solution)/shard_map/pallas_call | solution.py:225
  26.8 0.0 collective-permute-done.up_ref
  26.8 0.0 collective-permute-done.1.down_ref
  26.8 3.0 %shard_map.79 = f32[32,16,128]{2,1,0:T(8,128)S(1)} custom-call(bf16[1024,256]{1,0:T(8,128)(2,1)S(1)} %get-tuple-element.8.v, f32[16,2048]{1,0:T(8,128)S(1)} %get-tuple-element.9.cell_ref, bf16[256,3072]{1,0:T(8,128)(2,1)S(1)} %get-tuple-element.10.pick, f32[8,3072]{1,0:T(8,128)S(1)} %get-tuple-element.11.freqs, f32[64,2048]{1,0:T(8,128)S(1)} %get-tuple-element.12.field, ...), custom_call_target="tpu_custom_call" | custom-call | tf_op jit(solution)/shard_map/pallas_call | solution.py:240
  29.8 27.0 %all_to_all.20.parts_ref = f32[32,16,128]{2,1,0:T(8,128)S(1)} all-to-all(f32[32,16,128]{2,1,0:T(8,128)S(1)} %shard_map.79), channel_id=1, replica_groups=mesh['mp'=32,'dp'=16] {'mp'}, dimensions={0} | all-to-all | bytes 524288 | tf_op jit(solution)/shard_map/all_to_all | solution.py:251
  56.7 0.1 shard_map.80
  56.8 14.9 %all_to_all.21.upd_ref = bf16[32,16,128]{2,1,0:T(8,128)(2,1)S(1)} all-to-all(bf16[32,16,128]{2,1,0:T(8,128)(2,1)S(1)} %shard_map.80), channel_id=1, replica_groups=mesh['mp'=32,'dp'=16] {'mp'}, dimensions={0} | all-to-all | bytes 262144 | tf_op jit(solution)/shard_map/all_to_all | solution.py:253
  71.7 3.0 %shard_map.81 = bf16[16,48,128]{2,1,0:T(8,128)(2,1)S(1)} custom-call(bf16[32,16,128]{2,1,0:T(8,128)(2,1)S(1)} %all_to_all.21.upd_ref, bf16[256,3072]{1,0:T(8,128)(2,1)S(1)} %get-tuple-element.10.pick, f32[8,3072]{1,0:T(8,128)S(1)} %get-tuple-element.11.freqs, f32[64,2048]{1,0:T(8,128)S(1)} %get-tuple-element.12.field, ...), custom_call_target="tpu_custom_call" | custom-call | tf_op jit(solution)/shard_map/pallas_call | solution.py:254
  74.7 17.3 %all_to_all.22.recv_ref = bf16[16,48,128]{2,1,0:T(8,128)(2,1)S(1)} all-to-all(bf16[16,48,128]{2,1,0:T(8,128)(2,1)S(1)} %shard_map.81), channel_id=1, replica_groups=mesh['mp'=32,'dp'=16] {'dp'}, dimensions={0} | all-to-all | bytes 393216 | tf_op jit(solution)/shard_map/all_to_all | solution.py:266
  92.0 0.9 shard_map.82
  (4 shorter events, 0.1 us)
Async XLA Ops:
  0.6 0.9 copy-start
  1.5 0.7 copy-start.1
  2.2 0.7 copy-start.2
  2.9 0.7 copy-start.3
  3.6 12.1 %copy-start.4 = (bf16[64,4,2048]{2,1,0:T(4,128)(2,1)S(1)}, bf16[64,4,2048]{2,1,0:T(4,128)(2,1)}, u32[]{:S(2)}) copy-start(bf16[64,4,2048]{2,1,0:T(4,128)(2,1)} %param.7) | copy-start | bytes 3145732
  4.5 19.6 %all-to-all-start = ((bf16[16,32,256]{2,1,0:T(8,128)(2,1)}), bf16[16,32,256]{2,1,0:T(8,128)(2,1)S(1)}, u32[]{:S(2)}, u32[]{:S(2)}) async-start(bf16[16,32,256]{2,1,0:T(8,128)(2,1)} %shard_map.77), calls=%async_computation | async-start | bytes 524288 | tf_op jit(solution)/shard_map/all_to_all | solution.py:224
  16.0 10.7 %collective-permute-start = (bf16[320,256]{1,0:T(8,128)(2,1)S(1)}, bf16[320,256]{1,0:T(8,128)(2,1)S(1)}, u32[]{:S(2)}, u32[]{:S(2)}) collective-permute-start(bf16[320,256]{1,0:T(8,128)(2,1)S(1)} %pad_maximum_fusion), channel_id=1, source_target_pairs={{0,16},{1,17},{2,18},{3,19},{4,20},{5,21},{6,22},{7,23},{8,24},{9,... | collective-permute-start | bytes 491528 | tf_op jit(solution)/shard_map/ppermute | solution.py:215
  17.7 9.1 %collective-permute-start.1 = (bf16[320,256]{1,0:T(8,128)(2,1)S(1)}, bf16[320,256]{1,0:T(8,128)(2,1)S(1)}, u32[]{:S(2)}, u32[]{:S(2)}) collective-permute-start(bf16[320,256]{1,0:T(8,128)(2,1)S(1)} %pad_maximum_fusion.1), channel_id=1, source_target_pairs={{16,0},{17,1},{18,2},{19,3},{20,4},{21,5},{22,6},{23,7},{24,8},{25... | collective-permute-start | bytes 491528 | tf_op jit(solution)/shard_map/ppermute | solution.py:216

commit v3 on v2

--- a/solution.py
+++ b/solution.py
@@ -30,47 +30,57 @@
     return [pl.BlockSpec(memory_space=pltpu.VMEM)] * n
 
 
-def pack_kernel(res_ref, coef_ref, rec_ref, freq_ref, out_ref, big, side):
+def pack_kernel(res_hbm, coef_hbm, rec_hbm, freq_hbm, out_ref, res_in, coef_in, rec_in, freq_in, sems, big, side):
+    pairs = ((res_hbm, res_in), (coef_hbm, coef_in), (rec_hbm, rec_in), (freq_hbm, freq_in))
+    copies = [pltpu.make_async_copy(src, dst, sems.at[i]) for i, (src, dst) in enumerate(pairs)]
+    for copy in copies:
+        copy.start()
     odd = lax.rem(lax.axis_index("dp"), 2) == 1
-    big[...] = jnp.zeros_like(big)
+    big[DATA:, :] = jnp.zeros((256 - DATA, RHS), F32)
     side[...] = jnp.zeros_like(side)
-    big[0:DATA, :] = res_ref[...].astype(F32)
-    coef = coef_ref[...]
-    hi = coef.astype(BF).astype(F32)
-    side[0:KC, 0:DATA] = hi
-    side[KC : 2 * KC, 0:DATA] = coef - hi
-    side[8:9, 0:DATA] = rec_ref[...].astype(F32)
-    side[9:10, 0:DATA] = freq_ref[...].astype(F32)
-
-    def place(v):
-        tail = v[:, 128:256]
-        tail = jnp.where(odd, pltpu.roll(tail, 64, 1), tail)
-        return jnp.concatenate([v[:, 0:128], tail], axis=1).astype(BF)
-
-    res = place(jnp.transpose(big[...]))
-    rest = place(side[...])
+    for copy in copies:
+        copy.wait()
+    big[0:DATA, :] = res_in[...].astype(F32)
+    side[0:KC, 0:DATA] = coef_in[...]
+    side[4:5, 0:DATA] = rec_in[...].astype(F32)
+    side[5:6, 0:DATA] = freq_in[...].astype(F32)
+    res = jnp.transpose(big[...])
+    head, tail = side[:, 0:128], pltpu.roll(side[:, 128:256], 64, 1)
     for b in range(BLOCKS):
-        out_ref[b, 0:Q, :] = res[b * Q : (b + 1) * Q]
-        out_ref[b, Q : 2 * Q, :] = rest
-
-
-def tile_of(recv_ref, t, lo):
-    if t < BLOCKS:
-        return recv_ref[t, lo : lo + 16, 0:128].astype(F32)
-    p = 2 * (t - BLOCKS)
-    return recv_ref[p, lo : lo + 16, 128:256].astype(F32) + recv_ref[p + 1, lo : lo + 16, 128:256].astype(F32)
-
-
-def pick_data(recv_ref, pick, freqs):
-    sub = lax.broadcasted_iota(jnp.int32, (8, 128), 0) // KC
+        mine = res[b * Q : (b + 1) * Q]
+        more = mine[:, 128:256]
+        more = jnp.concatenate([more[0:8] + tail, more[8:16]], axis=0)
+        more = jnp.where(odd, pltpu.roll(more, 64, 1), more)
+        out_ref[b] = jnp.concatenate([mine[:, 0:128], more, head], axis=0).astype(BF)
+
+
+def unpack(recv_ref, tiles_ref, side):
+    low = lax.broadcasted_iota(jnp.int32, (Q, 128), 1) < 64
+    for p in range(BLOCKS // 2):
+        even, odd = recv_ref[2 * p].astype(F32), recv_ref[2 * p + 1].astype(F32)
+        for i, piece in enumerate((even, odd)):
+            t = 2 * p + i
+            tiles_ref[t] = piece[0:Q]
+            side[:, t * 128 : (t + 1) * 128] = piece[2 * Q :]
+        t = BLOCKS + p
+        even, odd = even[Q : 2 * Q], odd[Q : 2 * Q]
+        tiles_ref[t] = jnp.where(low, even, odd)
+        side[:, t * 128 : (t + 1) * 128] = pltpu.roll(jnp.where(low[0:8], odd[0:8], even[0:8]), 64, 1)
+    for t in range(TILES, SLABS):
+        tiles_ref[t] = jnp.zeros((Q, 128), F32)
+
+
+def pick_data(side, pick, freqs):
+    row = lax.broadcasted_iota(jnp.int32, (8, 128), 0)
+    recs = [(row // KC + 2 * g).astype(F32) for g in range(RK // 8)]
     for t in range(TILES):
         at = slice(t * 128, (t + 1) * 128)
-        side = tile_of(recv_ref, t, Q)
-        coef = 0.5 * (side[0:8] + pltpu.roll(side[0:8], KC, 0))
-        rec = side[8:9]
-        freqs[:, at] = jnp.broadcast_to(side[9:10], (8, 128))
+        v = side[:, at]
+        coef = 0.5 * jnp.where(row < KC, v, pltpu.roll(v, KC, 0))
+        rec = jnp.broadcast_to(v[4:5], (8, 128))
+        freqs[:, at] = jnp.broadcast_to(v[5:6], (8, 128))
         for g in range(RK // 16):
-            two = [jnp.where(rec == (sub + 2 * (2 * g + i)).astype(F32), coef, 0.0) for i in range(2)]
+            two = [jnp.where(rec == recs[2 * g + i], coef, 0.0) for i in range(2)]
             pick[g * 16 : g * 16 + 16, at] = jnp.concatenate(two, axis=0).astype(BF)
 
 
@@ -119,13 +129,10 @@
     return smooth_rows(rows, j == 0, j == SLABS - 1)
 
 
-def back_kernel(recv_ref, adj_ref, fwd_ref, pick, freqs, tiles_ref, v, field, cell, z):
+def back_kernel(recv_ref, adj_ref, fwd_ref, pick, freqs, tiles_ref, v, field, cell, z, side):
+    unpack(recv_ref, tiles_ref, side)
+    pick_data(side, pick, freqs)
     field[...] = fwd_ref[...].astype(F32)
-    pick_data(recv_ref, pick, freqs)
-    for t in range(TILES):
-        tiles_ref[t] = tile_of(recv_ref, t, 0)
-    for t in range(TILES, SLABS):
-        tiles_ref[t] = jnp.zeros((Q, 128), F32)
     from_data(lambda t: tiles_ref[t], pick, freqs, z, v)
     center_cells(v, adj_ref, field, cell)
 
@@ -185,20 +192,23 @@
     from_data(lambda t: upd_ref[t].astype(F32), pick, freqs, z, v)
     center_cells(v, adj_ref, field, cell)
     rows = with_edges(v, up_ref, down_ref, edge, cell)
+    low = lax.broadcasted_iota(jnp.int32, (8, 128), 1) < 64
     for b in range(BLOCKS):
-        out_ref[b, 0:Q, :] = (rows[b] * (1.0 / math.sqrt(NDATA))).astype(BF)
-        out_ref[b, Q : 2 * Q, :] = upd_ref[b]
-        out_ref[b, 2 * Q : 3 * Q, :] = upd_ref[BLOCKS + b // 2]
+        tail = upd_ref[BLOCKS + b // 2].astype(F32)
+        turned = pltpu.roll(tail, 64, 1)
+        tail = jnp.where(low, tail[0:8], turned[8:16]) if b % 2 == 0 else jnp.where(low, turned[0:8], tail[8:16])
+        piece = [rows[b] * (1.0 / math.sqrt(NDATA)), upd_ref[b].astype(F32), tail]
+        out_ref[b] = jnp.concatenate(piece, axis=0).astype(BF)
 
 
 def finish_kernel(recv_ref, upd_ref, model_ref):
-    odd = lax.rem(lax.axis_index("dp"), 2) == 1
-    part = lambda i: jnp.concatenate([recv_ref[b, i * Q : (i + 1) * Q, :] for b in range(BLOCKS)], axis=0).astype(F32)
-    model_ref[...] = jnp.transpose(part(0))
-    upd_ref[0:128, :] = jnp.transpose(part(1)).astype(BF)
-    tail = part(2)
-    tail = jnp.where(odd, pltpu.roll(tail, 64, 1), tail)
-    upd_ref[128:DATA, :] = jnp.transpose(tail)[0:64].astype(BF)
+    pieces = [recv_ref[b].astype(F32) for b in range(BLOCKS)]
+    model_ref[...] = jnp.transpose(jnp.concatenate([p[0:Q] for p in pieces], axis=0))
+    upd_ref[0:128, :] = jnp.transpose(jnp.concatenate([p[Q : 2 * Q] for p in pieces], axis=0)).astype(BF)
+    tail = []
+    for p in pieces:
+        tail += [p[2 * Q :], pltpu.roll(p[2 * Q :], 64, 1)]
+    upd_ref[128:DATA, :] = jnp.transpose(jnp.concatenate(tail, axis=0))[0:64].astype(BF)
 
 
 def per_device(forward_fields, adjoint_fields, data_rec, data_freq, data_coef, residual_cols):
@@ -214,12 +224,21 @@
     ]
     up = lax.ppermute(send_down, ("mp", "dp"), to_next)
     down = lax.ppermute(send_up, ("mp", "dp"), [(b, a) for a, b in to_next])
-    packed = call(
+    packed = pl.pallas_call(
         pack_kernel,
-        out_shape=shape((BLOCKS, 2 * Q, 256), BF),
-        in_specs=whole(4),
+        compiler_params=pltpu.CompilerParams(vmem_limit_bytes=60 * 1024 * 1024),
+        out_shape=shape((BLOCKS, 2 * Q + 8, 128), BF),
+        in_specs=[pl.BlockSpec(memory_space=pl.ANY)] * 4,
         out_specs=whole(1)[0],
-        scratch_shapes=[pltpu.VMEM((256, RHS), F32), pltpu.VMEM((2 * KC + 8, 256), F32)],
+        scratch_shapes=[
+            pltpu.VMEM((DATA, RHS), BF),
+            pltpu.VMEM((KC, DATA), F32),
+            pltpu.VMEM((1, DATA), jnp.int32),
+            pltpu.VMEM((1, DATA), jnp.int32),
+            pltpu.SemaphoreType.DMA((4,)),
+            pltpu.VMEM((256, RHS), F32),
+            pltpu.VMEM((8, 256), F32),
+        ],
     )(residual_cols, data_coef.T, data_rec.reshape(1, DATA), data_freq.reshape(1, DATA))
     recv = lax.all_to_all(packed, ("mp", "dp"), 0, 0, axis_index_groups=NEAR)
     pick, freqs, tiles, v, field, cell = call(
@@ -234,7 +253,7 @@
         ],
         in_specs=whole(3),
         out_specs=whole(6),
-        scratch_shapes=[pltpu.VMEM((NFREQ * Q, NDATA), BF)],
+        scratch_shapes=[pltpu.VMEM((NFREQ * Q, NDATA), BF), pltpu.VMEM((8, NDATA), F32)],
         cost_estimate=pl.CostEstimate(flops=4 * 10**9, bytes_accessed=8 * 10**6, transcendentals=0),
     )(recv, adj, fwd)
     gram = call(
@@ -253,7 +272,7 @@
     update = lax.all_to_all(mine, "mp", 0, 0)
     rows = call(
         model_kernel,
-        out_shape=shape((BLOCKS, 3 * Q, 128), BF),
+        out_shape=shape((BLOCKS, 2 * Q + 8, 128), BF),
         in_specs=whole(7),
         out_specs=whole(1)[0],
         scratch_shapes=[

time: 93.3 us -> 91.1 us (0.976)
  local copies, waits for them, and re-layouts: 4.25 us -> 1.43 us
    unnamed x10 -> x2, local copies, waits for them, and re-layouts: 2.93 us -> 0.01 us
    reshape x1, local copies, waits for them, and re-layouts: 0.28 us -> 1.34 us  [per_device(): adj = adjoint_fields.reshape(RK, CELLS)]
    pallas_call x2, Pallas kernels: 3.86 us -> 4.81 us  [the longest x1 2.97 us: per_device(): call(model_kernel, out_shape=shape((BLOCKS, 2 * Q + 8, 128), BF), in_spec...]
    reshape x1, local copies, waits for them, and re-layouts: 1.01 us -> 0.06 us  [per_device(): fwd = forward_fields.reshape(FK, CELLS)]
  transfers between devices with their start and end apart: 3 -> 3, of which waited for: 1 -> 1; matrix products, arithmetic and copies ran while one was open for 1% -> 2% of each run, Pallas kernels for 3% -> 3%
where the time goes in v3:
time: 91.1 us; the launch traced here: 90.7 us
  blocking collectives  59.8 us (66%)
  starting transfers between devices  13.1 us (14%)
  Pallas kernels  11.3 us (12%)
  waiting for transfers between devices  4.21 us (5%)
  local copies, waits for them, and re-layouts  1.43 us (2%)
    all_to_all x1, blocking collectives, per_device(): parts = lax.all_to_all(gram, 'mp', 0, 0)  27.9 us
    all_to_all x1, blocking collectives, per_device(): last = lax.all_to_all(rows, 'dp', 0, 0)  17 us
    all_to_all x1, blocking collectives, per_device(): update = lax.all_to_all(mine, 'mp', 0, 0)  14.9 us
    all_to_all x1, starting transfers between devices, per_device(): recv = lax.all_to_all(packed, ('mp', 'dp'), 0, 0, axis_index_groups=NEAR)  10.2 us
    all_to_all x1, waiting for transfers between devices, per_device(): recv = lax.all_to_all(packed, ('mp', 'dp'), 0, 0, axis_index_groups=NEAR)  4.21 us
    pallas_call x1, Pallas kernels, per_device(): call(gram_kernel, out_shape=shape((SLABS, Q, 128), F32), in_specs=whole(8...  2.97 us
    pallas_call x1, Pallas kernels, per_device(): call(model_kernel, out_shape=shape((BLOCKS, 2 * Q + 8, 128), BF), in_spec...  2.97 us
    pallas_call x1, Pallas kernels, per_device(): call(back_kernel, out_shape=[shape((RK, NDATA), BF), shape((8, NDATA), F3...  2.65 us
  transfers between devices with their start and end apart: 3, of which 1 were waited for; matrix products, arithmetic and copies ran while one was open for 2% of the time, Pallas kernels for 3%

profile of v3, /device:TPU:1, one launch (start us, length us, event | category | flops | bytes accessed | tf_op | source)
XLA Modules:
  0.0 90.7 jit_solution(13154597097255894944)
XLA Ops:
  0.6 0.0 copy-start
  0.6 1.8 %shard_map.77 = bf16[16,40,128]{2,1,0:T(8,128)(2,1)} custom-call(bf16[192,256]{1,0:T(8,128)(2,1)} %res_hbm.1, f32[4,192]{1,0:T(4,128)} %bitcast.3, s32[1,192]{1,0:T(1,128)} %bitcast.4, s32[1,192]{1,0:T(1,128)} %bitcast.5), custom_call_target="tpu_custom_call" | custom-call | tf_op jit(solution)/shard_map/pallas_call | solution.py:227
  2.5 10.2 %all-to-all-start = ((bf16[16,40,128]{2,1,0:T(8,128)(2,1)}), bf16[16,40,128]{2,1,0:T(8,128)(2,1)S(1)}, u32[]{:S(2)}, u32[]{:S(2)}) async-start(bf16[16,40,128]{2,1,0:T(8,128)(2,1)} %shard_map.77), calls=%async_computation | async-start | bytes 327680 | tf_op jit(solution)/shard_map/all_to_all | solution.py:243
  12.7 1.3 %reshape.18.adj_ref = bf16[256,2048]{1,0:T(8,128)(2,1)S(1)} reshape(bf16[64,4,2048]{2,1,0:T(4,128)(2,1)} %param.7) | data formatting | bytes 2097152 | tf_op jit(solution)/shard_map/reshape | solution.py:218
  14.0 0.0 copy-done
  14.0 0.1 reshape.19.fwd_ref
  14.2 1.7 %collective-permute-start = (bf16[320,256]{1,0:T(8,128)(2,1)S(1)}, bf16[320,256]{1,0:T(8,128)(2,1)S(1)}, u32[]{:S(2)}, u32[]{:S(2)}) collective-permute-start(bf16[320,256]{1,0:T(8,128)(2,1)S(1)} %pad_maximum_fusion), channel_id=1, source_target_pairs={{0,16},{1,17},{2,18},{3,19},{4,20},{5,21},{6,22},{7,23},{8,24},{9,... | collective-permute-start | bytes 491528 | tf_op jit(solution)/shard_map/ppermute | solution.py:225
  15.9 1.3 %collective-permute-start.1 = (bf16[320,256]{1,0:T(8,128)(2,1)S(1)}, bf16[320,256]{1,0:T(8,128)(2,1)S(1)}, u32[]{:S(2)}, u32[]{:S(2)}) collective-permute-start(bf16[320,256]{1,0:T(8,128)(2,1)S(1)} %pad_maximum_fusion.1), channel_id=1, source_target_pairs={{16,0},{17,1},{18,2},{19,3},{20,4},{21,5},{22,6},{23,7},{24,8},{25... | collective-permute-start | bytes 491528 | tf_op jit(solution)/shard_map/ppermute | solution.py:226
  17.2 4.2 %all-to-all-done.recv_ref = bf16[16,40,128]{2,1,0:T(8,128)(2,1)S(1)} async-done(((bf16[16,40,128]{2,1,0:T(8,128)(2,1)}), bf16[16,40,128]{2,1,0:T(8,128)(2,1)S(1)}, u32[]{:S(2)}, u32[]{:S(2)}) %all-to-all-start) | async-done | bytes 163872 | tf_op jit(solution)/shard_map/all_to_all | solution.py:243
  21.4 2.7 %shard_map.78 = (bf16[256,3072]{1,0:T(8,128)(2,1)S(1)}, f32[8,3072]{1,0:T(8,128)S(1)}, f32[32,16,128]{2,1,0:T(8,128)S(1)}, bf16[1024,256]{1,0:T(8,128)(2,1)S(1)}...) custom-call(bf16[16,40,128]{2,1,0:T(8,128)(2,1)S(1)} %all-to-all-done.recv_ref, bf16[256,2048]{1,0:T(8,128)(2,1)S(1)} %reshape.18.adj_ref, ...), custom_call_target="tpu_custom_call" | custom-call | flops 4000000000 | bytes 8000000 | tf_op jit(solution)/shard_map/pallas_call | solution.py:244
  24.0 0.0 collective-permute-done.up_ref
  24.0 0.0 collective-permute-done.1.down_ref
  24.0 3.0 %shard_map.79 = f32[32,16,128]{2,1,0:T(8,128)S(1)} custom-call(bf16[1024,256]{1,0:T(8,128)(2,1)S(1)} %get-tuple-element.8.v, f32[16,2048]{1,0:T(8,128)S(1)} %get-tuple-element.9.cell_ref, bf16[256,3072]{1,0:T(8,128)(2,1)S(1)} %get-tuple-element.10.pick, f32[8,3072]{1,0:T(8,128)S(1)} %get-tuple-element.11.freqs, f32[64,2048]{1,0:T(8,128)S(1)} %get-tuple-element.12.field, ...), custom_call_target="tpu_custom_call" | custom-call | tf_op jit(solution)/shard_map/pallas_call | solution.py:259
  27.0 27.9 %all_to_all.20.parts_ref = f32[32,16,128]{2,1,0:T(8,128)S(1)} all-to-all(f32[32,16,128]{2,1,0:T(8,128)S(1)} %shard_map.79), channel_id=1, replica_groups=mesh['mp'=32,'dp'=16] {'mp'}, dimensions={0} | all-to-all | bytes 524288 | tf_op jit(solution)/shard_map/all_to_all | solution.py:270
  54.9 0.1 shard_map.80
  54.9 14.9 %all_to_all.21.upd_ref = bf16[32,16,128]{2,1,0:T(8,128)(2,1)S(1)} all-to-all(bf16[32,16,128]{2,1,0:T(8,128)(2,1)S(1)} %shard_map.80), channel_id=1, replica_groups=mesh['mp'=32,'dp'=16] {'mp'}, dimensions={0} | all-to-all | bytes 262144 | tf_op jit(solution)/shard_map/all_to_all | solution.py:272
  69.9 3.0 %shard_map.81 = bf16[16,40,128]{2,1,0:T(8,128)(2,1)S(1)} custom-call(bf16[32,16,128]{2,1,0:T(8,128)(2,1)S(1)} %all_to_all.21.upd_ref, bf16[256,3072]{1,0:T(8,128)(2,1)S(1)} %get-tuple-element.10.pick, f32[8,3072]{1,0:T(8,128)S(1)} %get-tuple-element.11.freqs, f32[64,2048]{1,0:T(8,128)S(1)} %get-tuple-element.12.field, ...), custom_call_target="tpu_custom_call" | custom-call | tf_op jit(solution)/shard_map/pallas_call | solution.py:273
  72.9 17.0 %all_to_all.22.recv_ref = bf16[16,40,128]{2,1,0:T(8,128)(2,1)S(1)} all-to-all(bf16[16,40,128]{2,1,0:T(8,128)(2,1)S(1)} %shard_map.81), channel_id=1, replica_groups=mesh['mp'=32,'dp'=16] {'dp'}, dimensions={0} | all-to-all | bytes 327680 | tf_op jit(solution)/shard_map/all_to_all | solution.py:285
  89.9 0.8 shard_map.82
  (4 shorter events, 0.1 us)
Async XLA Ops:
  0.6 13.4 %copy-start = (bf16[16,4,2048]{2,1,0:T(4,128)(2,1)S(1)}, bf16[16,4,2048]{2,1,0:T(4,128)(2,1)}, u32[]{:S(2)}) copy-start(bf16[16,4,2048]{2,1,0:T(4,128)(2,1)} %param.6) | copy-start | bytes 786436
  2.5 18.9 %all-to-all-start = ((bf16[16,40,128]{2,1,0:T(8,128)(2,1)}), bf16[16,40,128]{2,1,0:T(8,128)(2,1)S(1)}, u32[]{:S(2)}, u32[]{:S(2)}) async-start(bf16[16,40,128]{2,1,0:T(8,128)(2,1)} %shard_map.77), calls=%async_computation | async-start | bytes 327680 | tf_op jit(solution)/shard_map/all_to_all | solution.py:243
  14.2 9.9 %collective-permute-start = (bf16[320,256]{1,0:T(8,128)(2,1)S(1)}, bf16[320,256]{1,0:T(8,128)(2,1)S(1)}, u32[]{:S(2)}, u32[]{:S(2)}) collective-permute-start(bf16[320,256]{1,0:T(8,128)(2,1)S(1)} %pad_maximum_fusion), channel_id=1, source_target_pairs={{0,16},{1,17},{2,18},{3,19},{4,20},{5,21},{6,22},{7,23},{8,24},{9,... | collective-permute-start | bytes 491528 | tf_op jit(solution)/shard_map/ppermute | solution.py:225
  15.9 8.2 %collective-permute-start.1 = (bf16[320,256]{1,0:T(8,128)(2,1)S(1)}, bf16[320,256]{1,0:T(8,128)(2,1)S(1)}, u32[]{:S(2)}, u32[]{:S(2)}) collective-permute-start(bf16[320,256]{1,0:T(8,128)(2,1)S(1)} %pad_maximum_fusion.1), channel_id=1, source_target_pairs={{16,0},{17,1},{18,2},{19,3},{20,4},{21,5},{22,6},{23,7},{24,8},{25... | collective-permute-start | bytes 491528 | tf_op jit(solution)/shard_map/ppermute | solution.py:226

commit v4 on v3

--- a/solution.py
+++ b/solution.py
@@ -24,6 +24,9 @@
 NEAR = [
     [(j if i & 2 == 0 else j ^ 2) * BLOCKS + i for i in range(BLOCKS)] for j in range(SLABS)
 ]
+
+
+ALONG_Z = [[z * 4 + y for z in range(8)] for y in range(4)]
 
 
 def whole(n):
@@ -155,10 +158,8 @@
         g = jnp.zeros((Q, 256), F32)
         for f in range(NFREQ):
             g = jnp.where(freq == float(f), u[f * Q : (f + 1) * Q], g)
-        gram_ref[2 * i] = g[:, 0:128]
-        gram_ref[2 * i + 1] = g[:, 128:256]
-    for t in range(TILES, SLABS):
-        gram_ref[t] = jnp.zeros((Q, 128), F32)
+        gram_ref[2 * i] = g[:, 0:128].astype(BF)
+        gram_ref[2 * i + 1] = g[:, 128:256].astype(BF)
 
 
 def smooth_rows(rows, first, last):
@@ -179,25 +180,29 @@
     return sweep(once)
 
 
-def update_kernel(parts_ref, tiles_ref, out_ref):
-    total = tiles_ref[lax.axis_index("mp")]
-    for j in range(SLABS):
-        total = total + parts_ref[j]
+def update_kernel(parts_ref, out_ref):
+    total = parts_ref[0].astype(F32)
+    for z in range(1, 8):
+        total = total + parts_ref[z].astype(F32)
     total = total.astype(BF)
     for j in range(SLABS):
         out_ref[j] = total
 
 
-def model_kernel(upd_ref, pick, freqs, field, adj_ref, up_ref, down_ref, out_ref, z, v, cell, edge):
-    from_data(lambda t: upd_ref[t].astype(F32), pick, freqs, z, v)
+def model_kernel(sums_ref, tiles_ref, pick, freqs, field, adj_ref, up_ref, down_ref, out_ref, z, v, cell, edge, upd_ref):
+    for t in range(TILES):
+        at = slice((t % 3) * Q, (t % 3 + 1) * Q)
+        part = [sums_ref[(t // 3) * 4 + y, at, :].astype(F32) for y in range(4)]
+        upd_ref[t] = (((part[0] + part[1]) + (part[2] + part[3])) + tiles_ref[t]).astype(BF).astype(F32)
+    from_data(lambda t: upd_ref[t], pick, freqs, z, v)
     center_cells(v, adj_ref, field, cell)
     rows = with_edges(v, up_ref, down_ref, edge, cell)
     low = lax.broadcasted_iota(jnp.int32, (8, 128), 1) < 64
     for b in range(BLOCKS):
-        tail = upd_ref[BLOCKS + b // 2].astype(F32)
+        tail = upd_ref[BLOCKS + b // 2]
         turned = pltpu.roll(tail, 64, 1)
         tail = jnp.where(low, tail[0:8], turned[8:16]) if b % 2 == 0 else jnp.where(low, turned[0:8], tail[8:16])
-        piece = [rows[b] * (1.0 / math.sqrt(NDATA)), upd_ref[b].astype(F32), tail]
+        piece = [rows[b] * (1.0 / math.sqrt(NDATA)), upd_ref[b], tail]
         out_ref[b] = jnp.concatenate(piece, axis=0).astype(BF)
 
 
@@ -258,7 +263,7 @@
     )(recv, adj, fwd)
     gram = call(
         gram_kernel,
-        out_shape=shape((SLABS, Q, 128), F32),
+        out_shape=shape((TILES, Q, 128), BF),
         in_specs=whole(8),
         out_specs=whole(1)[0],
         scratch_shapes=[
@@ -267,21 +272,22 @@
             pltpu.VMEM((NFREQ * Q, RK), BF),
         ],
     )(v, cell, pick, freqs, field, adj, up, down)
-    parts = lax.all_to_all(gram, "mp", 0, 0)
-    mine = call(update_kernel, out_shape=shape((SLABS, Q, 128), BF), in_specs=whole(2), out_specs=whole(1)[0])(parts, tiles)
+    parts = lax.all_to_all(gram.reshape(8, 3 * Q, 128), "mp", 0, 0, axis_index_groups=ALONG_Z)
+    mine = call(update_kernel, out_shape=shape((SLABS, 3 * Q, 128), BF), in_specs=whole(1), out_specs=whole(1)[0])(parts)
     update = lax.all_to_all(mine, "mp", 0, 0)
     rows = call(
         model_kernel,
         out_shape=shape((BLOCKS, 2 * Q + 8, 128), BF),
-        in_specs=whole(7),
+        in_specs=whole(8),
         out_specs=whole(1)[0],
         scratch_shapes=[
             pltpu.VMEM((NFREQ * Q, NDATA), BF),
             pltpu.VMEM((FK * Q, RK), BF),
             pltpu.VMEM((Q, CELLS), F32),
             pltpu.VMEM((FK, 2 * HALO), F32),
+            pltpu.VMEM((TILES, Q, 128), F32),
         ],
-    )(update, pick, freqs, field, adj, up, down)
+    )(update, tiles, pick, freqs, field, adj, up, down)
     last = lax.all_to_all(rows, "dp", 0, 0)
     return call(
         finish_kernel,

time: 91.1 us -> 88.5 us (0.971)
  blocking collectives: 59.8 us -> 56.7 us
    all_to_all x1, blocking collectives: 27.9 us -> 18.7 us  [per_device(): lax.all_to_all(gram.reshape(8, 3 * Q, 128), 'mp', 0, 0, axis_index_groups...]
    all_to_all x1, blocking collectives: 14.9 us -> 19.4 us  [per_device(): update = lax.all_to_all(mine, 'mp', 0, 0)]
    all_to_all x1, blocking collectives: 17 us -> 18.6 us  [per_device(): last = lax.all_to_all(rows, 'dp', 0, 0)]
where the time goes in v4:
time: 88.5 us; the launch traced here: 87.6 us
  blocking collectives  56.7 us (64%)
  starting transfers between devices  13.1 us (15%)
  Pallas kernels  11.3 us (13%)
  waiting for transfers between devices  4.21 us (5%)
  local copies, waits for them, and re-layouts  1.43 us (2%)
    all_to_all x1, blocking collectives, per_device(): update = lax.all_to_all(mine, 'mp', 0, 0)  19.4 us
    all_to_all x1, blocking collectives, per_device(): lax.all_to_all(gram.reshape(8, 3 * Q, 128), 'mp', 0, 0, axis_index_groups...  18.7 us
    all_to_all x1, blocking collectives, per_device(): last = lax.all_to_all(rows, 'dp', 0, 0)  18.6 us
    all_to_all x1, starting transfers between devices, per_device(): recv = lax.all_to_all(packed, ('mp', 'dp'), 0, 0, axis_index_groups=NEAR)  10.2 us
    all_to_all x1, waiting for transfers between devices, per_device(): recv = lax.all_to_all(packed, ('mp', 'dp'), 0, 0, axis_index_groups=NEAR)  4.21 us
    pallas_call x1, Pallas kernels, per_device(): call(model_kernel, out_shape=shape((BLOCKS, 2 * Q + 8, 128), BF), in_spec...  2.98 us
    pallas_call x1, Pallas kernels, per_device(): call(gram_kernel, out_shape=shape((TILES, Q, 128), BF), in_specs=whole(8)...  2.97 us
    pallas_call x1, Pallas kernels, per_device(): call(back_kernel, out_shape=[shape((RK, NDATA), BF), shape((8, NDATA), F3...  2.65 us
  transfers between devices with their start and end apart: 3, of which 1 were waited for; matrix products, arithmetic and copies ran while one was open for 2% of the time, Pallas kernels for 3%

profile of v4, /device:TPU:1, one launch (start us, length us, event | category | flops | bytes accessed | tf_op | source)
XLA Modules:
  0.0 87.6 jit_solution(12385332941787567365)
XLA Ops:
  0.6 0.0 copy-start
  0.6 1.8 %shard_map.77 = bf16[16,40,128]{2,1,0:T(8,128)(2,1)} custom-call(bf16[192,256]{1,0:T(8,128)(2,1)} %res_hbm.1, f32[4,192]{1,0:T(4,128)} %bitcast.5, s32[1,192]{1,0:T(1,128)} %bitcast.6, s32[1,192]{1,0:T(1,128)} %bitcast.7), custom_call_target="tpu_custom_call" | custom-call | tf_op jit(solution)/shard_map/pallas_call | solution.py:232
  2.5 10.2 %all-to-all-start = ((bf16[16,40,128]{2,1,0:T(8,128)(2,1)}), bf16[16,40,128]{2,1,0:T(8,128)(2,1)S(1)}, u32[]{:S(2)}, u32[]{:S(2)}) async-start(bf16[16,40,128]{2,1,0:T(8,128)(2,1)} %shard_map.77), calls=%async_computation | async-start | bytes 327680 | tf_op jit(solution)/shard_map/all_to_all | solution.py:248
  12.7 1.3 %reshape.21.adj_ref = bf16[256,2048]{1,0:T(8,128)(2,1)S(1)} reshape(bf16[64,4,2048]{2,1,0:T(4,128)(2,1)} %param.7) | data formatting | bytes 2097152 | tf_op jit(solution)/shard_map/reshape | solution.py:223
  14.0 0.0 copy-done
  14.0 0.1 reshape.22.fwd_ref
  14.2 1.7 %collective-permute-start = (bf16[320,256]{1,0:T(8,128)(2,1)S(1)}, bf16[320,256]{1,0:T(8,128)(2,1)S(1)}, u32[]{:S(2)}, u32[]{:S(2)}) collective-permute-start(bf16[320,256]{1,0:T(8,128)(2,1)S(1)} %pad_maximum_fusion), channel_id=1, source_target_pairs={{0,16},{1,17},{2,18},{3,19},{4,20},{5,21},{6,22},{7,23},{8,24},{9,... | collective-permute-start | bytes 491528 | tf_op jit(solution)/shard_map/ppermute | solution.py:230
  15.9 1.3 %collective-permute-start.1 = (bf16[320,256]{1,0:T(8,128)(2,1)S(1)}, bf16[320,256]{1,0:T(8,128)(2,1)S(1)}, u32[]{:S(2)}, u32[]{:S(2)}) collective-permute-start(bf16[320,256]{1,0:T(8,128)(2,1)S(1)} %pad_maximum_fusion.1), channel_id=1, source_target_pairs={{16,0},{17,1},{18,2},{19,3},{20,4},{21,5},{22,6},{23,7},{24,8},{25... | collective-permute-start | bytes 491528 | tf_op jit(solution)/shard_map/ppermute | solution.py:231
  17.2 4.2 %all-to-all-done.recv_ref = bf16[16,40,128]{2,1,0:T(8,128)(2,1)S(1)} async-done(((bf16[16,40,128]{2,1,0:T(8,128)(2,1)}), bf16[16,40,128]{2,1,0:T(8,128)(2,1)S(1)}, u32[]{:S(2)}, u32[]{:S(2)}) %all-to-all-start) | async-done | bytes 163872 | tf_op jit(solution)/shard_map/all_to_all | solution.py:248
  21.4 2.7 %shard_map.78 = (bf16[256,3072]{1,0:T(8,128)(2,1)S(1)}, f32[8,3072]{1,0:T(8,128)S(1)}, f32[32,16,128]{2,1,0:T(8,128)S(1)}, bf16[1024,256]{1,0:T(8,128)(2,1)S(1)}...) custom-call(bf16[16,40,128]{2,1,0:T(8,128)(2,1)S(1)} %all-to-all-done.recv_ref, bf16[256,2048]{1,0:T(8,128)(2,1)S(1)} %reshape.21.adj_ref, ...), custom_call_target="tpu_custom_call" | custom-call | flops 4000000000 | bytes 8000000 | tf_op jit(solution)/shard_map/pallas_call | solution.py:249
  24.0 0.0 collective-permute-done.up_ref
  24.0 0.0 collective-permute-done.1.down_ref
  24.0 3.0 %shard_map.79 = bf16[24,16,128]{2,1,0:T(8,128)(2,1)S(1)} custom-call(bf16[1024,256]{1,0:T(8,128)(2,1)S(1)} %get-tuple-element.8.v, f32[16,2048]{1,0:T(8,128)S(1)} %get-tuple-element.9.cell_ref, bf16[256,3072]{1,0:T(8,128)(2,1)S(1)} %get-tuple-element.10.pick, f32[8,3072]{1,0:T(8,128)S(1)} %get-tuple-element.11.freqs, ...), custom_call_target="tpu_custom_call" | custom-call | tf_op jit(solution)/shard_map/pallas_call | solution.py:264
  27.0 18.7 %all_to_all.20.parts_ref = bf16[8,48,128]{2,1,0:T(8,128)(2,1)S(1)} all-to-all(bf16[8,48,128]{2,1,0:T(8,128)(2,1)S(1)} %bitcast.4), channel_id=1, replica_groups={{0,64,128,192,256,320,384,448},{16,80,144,208,272,336,400,464},{32,96,1..., dimensions={0} | all-to-all | bytes 196608 | tf_op jit(solution)/shard_map/all_to_all | solution.py:275
  45.8 19.4 %all_to_all.21.sums_ref = bf16[32,48,128]{2,1,0:T(8,128)(2,1)S(1)} all-to-all(bf16[32,48,128]{2,1,0:T(8,128)(2,1)S(1)} %shard_map.80), channel_id=1, replica_groups=mesh['mp'=32,'dp'=16] {'mp'}, dimensions={0} | all-to-all | bytes 786432 | tf_op jit(solution)/shard_map/all_to_all | solution.py:277
  65.2 3.0 %shard_map.81 = bf16[16,40,128]{2,1,0:T(8,128)(2,1)S(1)} custom-call(bf16[32,48,128]{2,1,0:T(8,128)(2,1)S(1)} %all_to_all.21.sums_ref, f32[32,16,128]{2,1,0:T(8,128)S(1)} %get-tuple-element.13.tiles_ref, bf16[256,3072]{1,0:T(8,128)(2,1)S(1)} %get-tuple-element.10.pick, f32[8,3072]{1,0:T(8,128)S(1)} %get-tuple-element.11.freqs, ...), custom_call_target="tpu_custom_call" | custom-call | tf_op jit(solution)/shard_map/pallas_call | solution.py:278
  68.1 18.6 %all_to_all.22.recv_ref = bf16[16,40,128]{2,1,0:T(8,128)(2,1)S(1)} all-to-all(bf16[16,40,128]{2,1,0:T(8,128)(2,1)S(1)} %shard_map.81), channel_id=1, replica_groups=mesh['mp'=32,'dp'=16] {'dp'}, dimensions={0} | all-to-all | bytes 327680 | tf_op jit(solution)/shard_map/all_to_all | solution.py:291
  86.8 0.8 shard_map.82
  (5 shorter events, 0.1 us)
Async XLA Ops:
  0.6 13.4 %copy-start = (bf16[16,4,2048]{2,1,0:T(4,128)(2,1)S(1)}, bf16[16,4,2048]{2,1,0:T(4,128)(2,1)}, u32[]{:S(2)}) copy-start(bf16[16,4,2048]{2,1,0:T(4,128)(2,1)} %param.6) | copy-start | bytes 786436
  2.5 18.9 %all-to-all-start = ((bf16[16,40,128]{2,1,0:T(8,128)(2,1)}), bf16[16,40,128]{2,1,0:T(8,128)(2,1)S(1)}, u32[]{:S(2)}, u32[]{:S(2)}) async-start(bf16[16,40,128]{2,1,0:T(8,128)(2,1)} %shard_map.77), calls=%async_computation | async-start | bytes 327680 | tf_op jit(solution)/shard_map/all_to_all | solution.py:248
  14.2 9.9 %collective-permute-start = (bf16[320,256]{1,0:T(8,128)(2,1)S(1)}, bf16[320,256]{1,0:T(8,128)(2,1)S(1)}, u32[]{:S(2)}, u32[]{:S(2)}) collective-permute-start(bf16[320,256]{1,0:T(8,128)(2,1)S(1)} %pad_maximum_fusion), channel_id=1, source_target_pairs={{0,16},{1,17},{2,18},{3,19},{4,20},{5,21},{6,22},{7,23},{8,24},{9,... | collective-permute-start | bytes 491528 | tf_op jit(solution)/shard_map/ppermute | solution.py:230
  15.9 8.2 %collective-permute-start.1 = (bf16[320,256]{1,0:T(8,128)(2,1)S(1)}, bf16[320,256]{1,0:T(8,128)(2,1)S(1)}, u32[]{:S(2)}, u32[]{:S(2)}) collective-permute-start(bf16[320,256]{1,0:T(8,128)(2,1)S(1)} %pad_maximum_fusion.1), channel_id=1, source_target_pairs={{16,0},{17,1},{18,2},{19,3},{20,4},{21,5},{22,6},{23,7},{24,8},{25... | collective-permute-start | bytes 491528 | tf_op jit(solution)/shard_map/ppermute | solution.py:231

commit v5 on v4

--- a/solution.py
+++ b/solution.py
@@ -73,10 +73,10 @@
         tiles_ref[t] = jnp.zeros((Q, 128), F32)
 
 
-def pick_data(side, pick, freqs):
+def pick_data(side, pick, freqs, tiles):
     row = lax.broadcasted_iota(jnp.int32, (8, 128), 0)
     recs = [(row // KC + 2 * g).astype(F32) for g in range(RK // 8)]
-    for t in range(TILES):
+    for t in tiles:
         at = slice(t * 128, (t + 1) * 128)
         v = side[:, at]
         coef = 0.5 * jnp.where(row < KC, v, pltpu.roll(v, KC, 0))
@@ -92,14 +92,19 @@
     return jnp.where(lane == k, v, 0.0)
 
 
-def from_data(tiles, pick, freqs, z, v):
-    for t in range(TILES):
-        at = slice(t * 128, (t + 1) * 128)
-        x = tiles(t)
-        freq = jnp.concatenate([freqs[:, at], freqs[:, at]], axis=0)
-        for f in range(NFREQ):
-            z[f * Q : (f + 1) * Q, at] = jnp.where(freq == float(f), x, 0.0).astype(BF)
-    w = lax.dot_general(z[...], pick[...], NT, preferred_element_type=F32)
+def from_data(tiles, pick, freqs, z, v, prepare=lambda group: None):
+    w = jnp.zeros((NFREQ * Q, RK), F32)
+    for start in range(0, TILES, 6):
+        group = range(start, start + 6)
+        prepare(group)
+        for t in group:
+            at = slice(t * 128, (t + 1) * 128)
+            x = tiles(t)
+            freq = jnp.concatenate([freqs[:, at], freqs[:, at]], axis=0)
+            for f in range(NFREQ):
+                z[f * Q : (f + 1) * Q, at] = jnp.where(freq == float(f), x, 0.0).astype(BF)
+        at = slice(start * 128, (start + 6) * 128)
+        w = w + lax.dot_general(z[:, at], pick[:, at], NT, preferred_element_type=F32)
     for f in range(NFREQ):
         for k in range(KC):
             fk = f * KC + k
@@ -134,9 +139,8 @@
 
 def back_kernel(recv_ref, adj_ref, fwd_ref, pick, freqs, tiles_ref, v, field, cell, z, side):
     unpack(recv_ref, tiles_ref, side)
-    pick_data(side, pick, freqs)
     field[...] = fwd_ref[...].astype(F32)
-    from_data(lambda t: tiles_ref[t], pick, freqs, z, v)
+    from_data(lambda t: tiles_ref[t], pick, freqs, z, v, lambda group: pick_data(side, pick, freqs, group))
     center_cells(v, adj_ref, field, cell)
 
 

time: 88.5 us -> 88.5 us (level)
  no operation moved by 1% of the time
where the time goes in v5:
time: 88.5 us; the launch traced here: 87.6 us
  blocking collectives  56.7 us (64%)
  starting transfers between devices  13.1 us (15%)
  Pallas kernels  11.3 us (13%)
  waiting for transfers between devices  4.21 us (5%)
  local copies, waits for them, and re-layouts  1.43 us (2%)
    all_to_all x1, blocking collectives, per_device(): update = lax.all_to_all(mine, 'mp', 0, 0)  19.4 us
    all_to_all x1, blocking collectives, per_device(): lax.all_to_all(gram.reshape(8, 3 * Q, 128), 'mp', 0, 0, axis_index_groups...  18.7 us
    all_to_all x1, blocking collectives, per_device(): last = lax.all_to_all(rows, 'dp', 0, 0)  18.6 us
    all_to_all x1, starting transfers between devices, per_device(): recv = lax.all_to_all(packed, ('mp', 'dp'), 0, 0, axis_index_groups=NEAR)  10.2 us
    all_to_all x1, waiting for transfers between devices, per_device(): recv = lax.all_to_all(packed, ('mp', 'dp'), 0, 0, axis_index_groups=NEAR)  4.21 us
    pallas_call x1, Pallas kernels, per_device(): call(model_kernel, out_shape=shape((BLOCKS, 2 * Q + 8, 128), BF), in_spec...  2.98 us
    pallas_call x1, Pallas kernels, per_device(): call(gram_kernel, out_shape=shape((TILES, Q, 128), BF), in_specs=whole(8)...  2.97 us
    pallas_call x1, Pallas kernels, per_device(): call(back_kernel, out_shape=[shape((RK, NDATA), BF), shape((8, NDATA), F3...  2.65 us
  transfers between devices with their start and end apart: 3, of which 1 were waited for; matrix products, arithmetic and copies ran while one was open for 2% of the time, Pallas kernels for 3%

profile of v5, /device:TPU:1, one launch (start us, length us, event | category | flops | bytes accessed | tf_op | source)
XLA Modules:
  0.0 87.6 jit_solution(15783630880912445413)
XLA Ops:
  0.6 0.0 copy-start
  0.6 1.8 %shard_map.77 = bf16[16,40,128]{2,1,0:T(8,128)(2,1)} custom-call(bf16[192,256]{1,0:T(8,128)(2,1)} %res_hbm.1, f32[4,192]{1,0:T(4,128)} %bitcast.5, s32[1,192]{1,0:T(1,128)} %bitcast.6, s32[1,192]{1,0:T(1,128)} %bitcast.7), custom_call_target="tpu_custom_call" | custom-call | tf_op jit(solution)/shard_map/pallas_call | solution.py:236
  2.5 10.2 %all-to-all-start = ((bf16[16,40,128]{2,1,0:T(8,128)(2,1)}), bf16[16,40,128]{2,1,0:T(8,128)(2,1)S(1)}, u32[]{:S(2)}, u32[]{:S(2)}) async-start(bf16[16,40,128]{2,1,0:T(8,128)(2,1)} %shard_map.77), calls=%async_computation | async-start | bytes 327680 | tf_op jit(solution)/shard_map/all_to_all | solution.py:252
  12.7 1.3 %reshape.21.adj_ref = bf16[256,2048]{1,0:T(8,128)(2,1)S(1)} reshape(bf16[64,4,2048]{2,1,0:T(4,128)(2,1)} %param.7) | data formatting | bytes 2097152 | tf_op jit(solution)/shard_map/reshape | solution.py:227
  14.0 0.0 copy-done
  14.0 0.1 reshape.22.fwd_ref
  14.2 1.7 %collective-permute-start = (bf16[320,256]{1,0:T(8,128)(2,1)S(1)}, bf16[320,256]{1,0:T(8,128)(2,1)S(1)}, u32[]{:S(2)}, u32[]{:S(2)}) collective-permute-start(bf16[320,256]{1,0:T(8,128)(2,1)S(1)} %pad_maximum_fusion), channel_id=1, source_target_pairs={{0,16},{1,17},{2,18},{3,19},{4,20},{5,21},{6,22},{7,23},{8,24},{9,... | collective-permute-start | bytes 491528 | tf_op jit(solution)/shard_map/ppermute | solution.py:234
  15.9 1.3 %collective-permute-start.1 = (bf16[320,256]{1,0:T(8,128)(2,1)S(1)}, bf16[320,256]{1,0:T(8,128)(2,1)S(1)}, u32[]{:S(2)}, u32[]{:S(2)}) collective-permute-start(bf16[320,256]{1,0:T(8,128)(2,1)S(1)} %pad_maximum_fusion.1), channel_id=1, source_target_pairs={{16,0},{17,1},{18,2},{19,3},{20,4},{21,5},{22,6},{23,7},{24,8},{25... | collective-permute-start | bytes 491528 | tf_op jit(solution)/shard_map/ppermute | solution.py:235
  17.2 4.2 %all-to-all-done.recv_ref = bf16[16,40,128]{2,1,0:T(8,128)(2,1)S(1)} async-done(((bf16[16,40,128]{2,1,0:T(8,128)(2,1)}), bf16[16,40,128]{2,1,0:T(8,128)(2,1)S(1)}, u32[]{:S(2)}, u32[]{:S(2)}) %all-to-all-start) | async-done | bytes 163872 | tf_op jit(solution)/shard_map/all_to_all | solution.py:252
  21.4 2.7 %shard_map.78 = (bf16[256,3072]{1,0:T(8,128)(2,1)S(1)}, f32[8,3072]{1,0:T(8,128)S(1)}, f32[32,16,128]{2,1,0:T(8,128)S(1)}, bf16[1024,256]{1,0:T(8,128)(2,1)S(1)}...) custom-call(bf16[16,40,128]{2,1,0:T(8,128)(2,1)S(1)} %all-to-all-done.recv_ref, bf16[256,2048]{1,0:T(8,128)(2,1)S(1)} %reshape.21.adj_ref, ...), custom_call_target="tpu_custom_call" | custom-call | flops 4000000000 | bytes 8000000 | tf_op jit(solution)/shard_map/pallas_call | solution.py:253
  24.0 0.0 collective-permute-done.up_ref
  24.0 0.0 collective-permute-done.1.down_ref
  24.0 3.0 %shard_map.79 = bf16[24,16,128]{2,1,0:T(8,128)(2,1)S(1)} custom-call(bf16[1024,256]{1,0:T(8,128)(2,1)S(1)} %get-tuple-element.8.v, f32[16,2048]{1,0:T(8,128)S(1)} %get-tuple-element.9.cell_ref, bf16[256,3072]{1,0:T(8,128)(2,1)S(1)} %get-tuple-element.10.pick, f32[8,3072]{1,0:T(8,128)S(1)} %get-tuple-element.11.freqs, ...), custom_call_target="tpu_custom_call" | custom-call | tf_op jit(solution)/shard_map/pallas_call | solution.py:268
  27.0 18.7 %all_to_all.20.parts_ref = bf16[8,48,128]{2,1,0:T(8,128)(2,1)S(1)} all-to-all(bf16[8,48,128]{2,1,0:T(8,128)(2,1)S(1)} %bitcast.4), channel_id=1, replica_groups={{0,64,128,192,256,320,384,448},{16,80,144,208,272,336,400,464},{32,96,1..., dimensions={0} | all-to-all | bytes 196608 | tf_op jit(solution)/shard_map/all_to_all | solution.py:279
  45.8 19.4 %all_to_all.21.sums_ref = bf16[32,48,128]{2,1,0:T(8,128)(2,1)S(1)} all-to-all(bf16[32,48,128]{2,1,0:T(8,128)(2,1)S(1)} %shard_map.80), channel_id=1, replica_groups=mesh['mp'=32,'dp'=16] {'mp'}, dimensions={0} | all-to-all | bytes 786432 | tf_op jit(solution)/shard_map/all_to_all | solution.py:281
  65.2 3.0 %shard_map.81 = bf16[16,40,128]{2,1,0:T(8,128)(2,1)S(1)} custom-call(bf16[32,48,128]{2,1,0:T(8,128)(2,1)S(1)} %all_to_all.21.sums_ref, f32[32,16,128]{2,1,0:T(8,128)S(1)} %get-tuple-element.13.tiles_ref, bf16[256,3072]{1,0:T(8,128)(2,1)S(1)} %get-tuple-element.10.pick, f32[8,3072]{1,0:T(8,128)S(1)} %get-tuple-element.11.freqs, ...), custom_call_target="tpu_custom_call" | custom-call | tf_op jit(solution)/shard_map/pallas_call | solution.py:282
  68.1 18.6 %all_to_all.22.recv_ref = bf16[16,40,128]{2,1,0:T(8,128)(2,1)S(1)} all-to-all(bf16[16,40,128]{2,1,0:T(8,128)(2,1)S(1)} %shard_map.81), channel_id=1, replica_groups=mesh['mp'=32,'dp'=16] {'dp'}, dimensions={0} | all-to-all | bytes 327680 | tf_op jit(solution)/shard_map/all_to_all | solution.py:295
  86.8 0.8 shard_map.82
  (5 shorter events, 0.1 us)
Async XLA Ops:
  0.6 13.4 %copy-start = (bf16[16,4,2048]{2,1,0:T(4,128)(2,1)S(1)}, bf16[16,4,2048]{2,1,0:T(4,128)(2,1)}, u32[]{:S(2)}) copy-start(bf16[16,4,2048]{2,1,0:T(4,128)(2,1)} %param.6) | copy-start | bytes 786436
  2.5 18.9 %all-to-all-start = ((bf16[16,40,128]{2,1,0:T(8,128)(2,1)}), bf16[16,40,128]{2,1,0:T(8,128)(2,1)S(1)}, u32[]{:S(2)}, u32[]{:S(2)}) async-start(bf16[16,40,128]{2,1,0:T(8,128)(2,1)} %shard_map.77), calls=%async_computation | async-start | bytes 327680 | tf_op jit(solution)/shard_map/all_to_all | solution.py:252
  14.2 9.9 %collective-permute-start = (bf16[320,256]{1,0:T(8,128)(2,1)S(1)}, bf16[320,256]{1,0:T(8,128)(2,1)S(1)}, u32[]{:S(2)}, u32[]{:S(2)}) collective-permute-start(bf16[320,256]{1,0:T(8,128)(2,1)S(1)} %pad_maximum_fusion), channel_id=1, source_target_pairs={{0,16},{1,17},{2,18},{3,19},{4,20},{5,21},{6,22},{7,23},{8,24},{9,... | collective-permute-start | bytes 491528 | tf_op jit(solution)/shard_map/ppermute | solution.py:234
  15.9 8.2 %collective-permute-start.1 = (bf16[320,256]{1,0:T(8,128)(2,1)S(1)}, bf16[320,256]{1,0:T(8,128)(2,1)S(1)}, u32[]{:S(2)}, u32[]{:S(2)}) collective-permute-start(bf16[320,256]{1,0:T(8,128)(2,1)S(1)} %pad_maximum_fusion.1), channel_id=1, source_target_pairs={{16,0},{17,1},{18,2},{19,3},{20,4},{21,5},{22,6},{23,7},{24,8},{25... | collective-permute-start | bytes 491528 | tf_op jit(solution)/shard_map/ppermute | solution.py:235
